TPU v7x, 128 devices: a whole 4x4x4 slice. The times are simulated.
128 devices in a mesh: gx: 4 (over x), gy: 32 (over y, z, core).
Axes of the slice: x: 4, y: 4, z: 4, core: 2. Of those that a mesh axis runs over, the one named last changes fastest.
Arguments:
- grid_scalars: float32 [54, 8, 64, 128], P(None, 'gx', 'gy'), may hold values from -6 to 6
- axial_speed: float32 [8, 64, 128], P('gx', 'gy'), may hold values from 0.1 to 0.4
- particles: float32 [54, 32, 65536], P(None, None, ('gx', 'gy')), may hold values from -6 to 6
- cell_owner: int32 [8, 64, 128], P('gx', 'gy'), may hold values from 0 to 31, as said below
- cell_slot: int32 [8, 64, 128], P('gx', 'gy'), may hold values from 0 to 511, as said below
- mix_rate: float32 [65536], P(('gx', 'gy')), may hold values from 0.2 to 0.6
- partner: int32 [32, 65536], P(None, ('gx', 'gy')), may hold values from 0 to 31, as said below
- chem_input: bfloat16 [256, 54], replicated, may hold values from -0.875 to 0.875
- chem_hidden: bfloat16 [256, 256], replicated, may hold values from -0.375 to 0.375
- chem_output: bfloat16 [54, 256], replicated, may hold values from -0.375 to 0.375
- react_slots: int32 [128, 256], P(('gx', 'gy')), may hold values from 0 to 511, as said below
- react_count: int32 [128], P(('gx', 'gy')), may hold values from 1 to 256, as said below
- leave_slots: int32 [128, 256], P(('gx', 'gy')), may hold values from 0 to 512, as said below
- arrive_slots: int32 [128, 256], P(('gx', 'gy')), may hold values from 0 to 512, as said below
Outputs:
- grid_out: float32 [54, 8, 64, 128], P(None, 'gx', 'gy')
- particles_out: float32 [54, 32, 65536], P(None, None, ('gx', 'gy'))
Inputs may be any that keep to these rules, and one draw needn't show every extreme that they name: `cell_owner`: within each gx index, each of the 32 owners holds exactly 512 cells of that gx index's grid boxes, each slot once; from one grid box to one owner go at most 24 cells, and exactly 24 for some pairs in every draw. `cell_slot`: slots as described for cell_owner. In each cell partner pairs the 32 particles: partner of partner is the particle itself, never itself. `react_slots`: distinct slots in each owner's row. `react_count`: some owner has 256 live entries in every draw. `leave_slots`: every device hands one or 2 cells to every device, 2 to some; the value 512 marks an empty place; the leaving slots of a device are distinct and are exactly the slots that arriving cells take there. `arrive_slots`: as for leave_slots.
All inputs are finite; a program needn't handle non-finite values.
Results may differ from a plain program's by a relative error of at most 0.0013.
Values sent between devices are 32-bit elements; how exact they have to be, the bound alone decides.
A program may use at most 128 MiB of HBM per device.

v0:
```python
import jax
import jax.numpy as jnp
from jax import lax
from jax.sharding import PartitionSpec as P

SUBSTEPS = 2


DIFFUSION = 0.1
PAIR_WEIGHT = 0.4


def with_halo(array, sides, width):
    edges = {}
    for axis, dim in sides:
        size, length = (lax.axis_size(axis), array.shape[dim])
        up = [(i, (i + 1) % size) for i in range(size - 1)]
        last = lax.slice_in_dim(array, length - width, length, axis=dim)
        first = lax.slice_in_dim(array, 0, width, axis=dim)
        edges[dim] = (
            lax.ppermute(last, axis, up),
            lax.ppermute(first, axis, [(b, a) for a, b in up]),
        )
    done = []
    for _, dim in sides:
        low, high = edges[dim]
        around = [(width, width) if d in done else (0, 0) for d in range(array.ndim)]
        array = jnp.concatenate([jnp.pad(low, around), array, jnp.pad(high, around)], axis=dim)
        done.append(dim)
    return array


def split_up(array, dim, size):
    shape = array.shape
    blocks = array.reshape(*shape[:dim], size, shape[dim] // size, *shape[dim + 1 :])
    return jnp.moveaxis(blocks, dim, 0)


def joined_along(blocks, dim):
    blocks = jnp.moveaxis(blocks, 0, dim)
    shape = blocks.shape
    return blocks.reshape(*shape[:dim], shape[dim] * shape[dim + 1], *shape[dim + 2 :])


def one_exchange(array, axis, axes, splits, concats):
    sizes = [lax.axis_size(a) for a in axes]
    blocks = split_up(array, splits[0], sizes[0])
    blocks = jnp.moveaxis(split_up(blocks, splits[1] + 1, sizes[1]), 0, 1)
    inside = blocks.shape[2:]
    blocks = blocks.reshape(-1, *inside)
    blocks = lax.all_to_all(blocks, axis, split_axis=0, concat_axis=0, tiled=True)
    blocks = joined_along(blocks.reshape(*sizes, *inside), concats[0] + 1)
    return joined_along(blocks, concats[1])


def advance(padded, axial_speed):
    center = padded[:, 1:-1, 1:-1, :]
    upstream = padded[:, :-2, 1:-1, :]
    beside = upstream + padded[:, 2:, 1:-1, :]
    beside = beside + padded[:, 1:-1, :-2, :] + padded[:, 1:-1, 2:, :]
    beside = beside + jnp.roll(center, 1, axis=3) + jnp.roll(center, -1, axis=3)
    return center + DIFFUSION * (beside - 6.0 * center) - axial_speed[None] * (center - upstream)


def particle_section(
    state,
    filtered,
    relaxation,
    partner,
    chem_input,
    chem_hidden,
    chem_output,
    chosen_slots,
    live_count,
):
    state = state + relaxation[None, None, :] * (filtered[:, None, :] - state)
    partner_state = jnp.take_along_axis(state, partner[None, :, :], axis=1)
    state = state + PAIR_WEIGHT * (partner_state - state)
    chosen = jnp.take(state, chosen_slots, axis=2)
    feed_rows = chosen.reshape(chosen.shape[0], -1).astype(jnp.bfloat16)
    layer_one = jax.nn.silu(
        jnp.dot(chem_input, feed_rows, preferred_element_type=jnp.float32)
    ).astype(jnp.bfloat16)
    layer_two = jax.nn.silu(
        jnp.dot(chem_hidden, layer_one, preferred_element_type=jnp.float32)
    ).astype(jnp.bfloat16)
    change = jnp.dot(chem_output, layer_two, preferred_element_type=jnp.float32).astype(
        jnp.bfloat16
    )
    change = change.reshape(chosen.shape).astype(jnp.float32)
    active = jnp.arange(chosen_slots.shape[0], dtype=jnp.int32) < live_count
    change = jnp.where(active[None, None, :], change, jnp.zeros_like(change))
    state = state.at[:, :, chosen_slots].add(change)
    source = (
        jnp.zeros(filtered.shape, filtered.dtype).at[:, chosen_slots].set(jnp.mean(change, axis=1))
    )
    return (state, source)


def per_device(
    grid_scalars,
    axial_speed,
    particles,
    cell_owner,
    cell_slot,
    mix_rate,
    partner,
    chem_input,
    chem_hidden,
    chem_output,
    react_slots,
    react_count,
    leave_slots,
    arrive_slots,
):
    scalar_count = grid_scalars.shape[0]
    cell_count = cell_owner.size
    lane_count = lax.axis_size("gy")
    owners_here = cell_owner.reshape(-1)
    slots_here = cell_slot.reshape(-1)
    capacity = 3 * (cell_count // lane_count) // 2
    onehot = (owners_here[:, None] == jnp.arange(lane_count, dtype=jnp.int32)[None, :]).astype(
        jnp.int32
    )
    ranking = jnp.sum(jnp.cumsum(onehot, axis=0) * onehot, axis=1) - 1
    places = owners_here * capacity + ranking
    source_cell = (
        jnp.full((lane_count * capacity,), cell_count, jnp.int32)
        .at[places]
        .set(jnp.arange(cell_count, dtype=jnp.int32))
    )
    labels = (
        jnp.full((1, lane_count * capacity), cell_count, jnp.int32).at[0, places].set(slots_here)
    )
    grid = grid_scalars
    state = particles
    for substep in range(SUBSTEPS):
        padded = with_halo(grid, (("gx", 1), ("gy", 2)), 1)
        grid = advance(padded, axial_speed)
        flattened = grid.reshape(scalar_count, cell_count)
        outgoing = jnp.take(flattened, source_cell, axis=1, mode="fill", fill_value=0.0)
        arrived, arrived_slots = (
            lax.all_to_all(outgoing, "gy", split_axis=1, concat_axis=1, tiled=True),
            lax.all_to_all(labels, "gy", split_axis=1, concat_axis=1, tiled=True),
        )
        landed = arrived_slots[0]
        filtered = (
            jnp.zeros((scalar_count, cell_count), jnp.float32)
            .at[:, landed]
            .set(arrived, mode="drop")
        )
        state, source = particle_section(
            state,
            filtered,
            mix_rate,
            partner,
            chem_input,
            chem_hidden,
            chem_output,
            react_slots[0],
            react_count[0],
        )
        returned = jnp.take(source, landed, axis=1, mode="fill", fill_value=0.0)
        homeward = lax.all_to_all(returned, "gy", split_axis=1, concat_axis=1, tiled=True)
        feedback = jnp.take(homeward, places, axis=1)
        grid = grid + feedback.reshape(grid.shape)
    flat_parts = state.reshape(scalar_count * state.shape[1], cell_count)
    outgoing_cells = jnp.take(flat_parts, leave_slots[0], axis=1, mode="fill", fill_value=0.0)
    group_count = lax.axis_size("gx")
    sectioned = outgoing_cells.reshape(flat_parts.shape[0], group_count, -1)
    arrived_cells = one_exchange(sectioned, ("gx", "gy"), ("gx", "gy"), (1, 2), (1, 2)).reshape(
        flat_parts.shape[0], -1
    )
    relocated = flat_parts.at[:, arrive_slots[0]].set(arrived_cells, mode="drop")
    return (grid, relocated.reshape(state.shape))


def solution(mesh):
    placed = (
        P(None, "gx", "gy", None),
        P("gx", "gy", None),
        P(None, None, ("gx", "gy")),
        P("gx", "gy", None),
        P("gx", "gy", None),
        P(("gx", "gy")),
        P(None, ("gx", "gy")),
        P(),
        P(),
        P(),
        P(("gx", "gy"), None),
        P(("gx", "gy")),
        P(("gx", "gy"), None),
        P(("gx", "gy"), None),
    )
    return jax.shard_map(
        per_device,
        mesh=mesh,
        in_specs=placed,
        out_specs=(P(None, "gx", "gy", None), P(None, None, ("gx", "gy"))),
        check_vma=False,
    )
```

profile of v0, /device:TPU:1, one launch (start us, length us, event | category | flops | bytes accessed | tf_op | source)
XLA Modules:
  0.0 872.3 jit_solution(600344486353750731)
XLA Ops:
  21.1 9.6 %all-to-all-start = ((s32[1,32,24]{2,0,1:T(1,128)}), s32[1,32,24]{2,0,1:T(1,128)S(1)}, u32[]{:S(2)}, u32[]{:S(2)}) async-start(s32[1,32,24]{2,0,1:T(1,128)} %bitcast.7), calls=%async_computation | async-start | bytes 32768 | tf_op jit(solution)/shard_map/all_to_all | solution.py:144
  47.5 7.4 all-to-all-start.1
  55.0 8.0 all-to-all-done.1
  69.4 4.6 multiply_add_fusion.1
  74.0 6.8 copy.95
  80.8 236.7 %gather_fusion.2 = f32[16384,54]{1,0:T(8,128)} fusion(f32[54,32,512]{0,2,1:T(8,128)} %copy.95, s32[16384]{0:T(1024)S(1)} %bitcast.188), kind=kCustom, calls=%fused_computation.1.clone | custom fusion | bytes 7208960 | tf_op jit(solution)/shard_map/jit(take_along_axis)/gather | solution.py:77
  317.5 7.1 copy.117
  324.6 6.2 fusion.5
  330.8 9.1 %copy.97 = f32[54,32,512]{0,1,2:T(8,128)} copy(f32[54,32,512]{2,1,0:T(8,128)} %fusion.5) | data formatting | bytes 7077888 | tf_op jit(solution)/shard_map/add | solution.py:78
  356.8 4.5 copy.99
  361.4 4.5 select_bitcast_fusion.1
  374.6 7.6 all-to-all-done.2
  401.1 7.6 all-to-all-start.3
  408.7 34.0 %scatter_fusion = f32[54,32,512]{0,1,2:T(8,128)} fusion(f32[54,32,512]{0,1,2:T(8,128)} %copy.97, s32[256]{0:T(256)S(1)} %bitcast.221, f32[256,54,32]{1,2,0:T(8,128)} %get-tuple-element.12), kind=kCustom, calls=%fused_computation.15 | custom fusion | flops 442368 | bytes 5309440 | tf_op jit(solution)/shard_map/scatter-add | solution.py:93
  442.7 7.3 copy.105
  455.8 4.7 multiply_add_fusion
  460.4 7.2 copy.106
  467.6 236.7 %gather_fusion.7 = f32[16384,54]{1,0:T(8,128)} fusion(f32[54,32,512]{0,2,1:T(8,128)} %copy.106, s32[16384]{0:T(1024)S(1)} %bitcast.189), kind=kCustom, calls=%fused_computation.7.clone | custom fusion | bytes 7208960 | tf_op jit(solution)/shard_map/jit(take_along_axis)/gather | solution.py:77
  704.3 7.2 copy.118
  711.5 6.2 fusion.3
  717.6 9.1 %copy.108 = f32[54,32,512]{0,1,2:T(8,128)} copy(f32[54,32,512]{2,1,0:T(8,128)} %fusion.3) | data formatting | bytes 7077888 | tf_op jit(solution)/shard_map/add | solution.py:78
  743.6 4.5 copy.110
  748.2 4.5 select_bitcast_fusion
  756.8 7.4 all-to-all-start.4
  764.1 34.0 %scatter_fusion.1 = f32[54,32,512]{0,1,2:T(8,128)} fusion(f32[54,32,512]{0,1,2:T(8,128)} %copy.108, s32[256]{0:T(256)S(1)} %bitcast.223, f32[256,54,32]{1,2,0:T(8,128)} %get-tuple-element.10), kind=kCustom, calls=%fused_computation.18 | custom fusion | flops 442368 | bytes 5309440 | tf_op jit(solution)/shard_map/scatter-add | solution.py:93
  798.1 7.3 copy.113
  805.5 5.0 copy.115
  810.5 5.3 gather_fusion
  819.9 10.4 %all-to-all-start.5 = ((f32[128,1728,1,2]{1,3,2,0:T(2,128)}), f32[128,1728,1,2]{1,3,2,0:T(2,128)S(1)}, u32[]{:S(2)}, u32[]{:S(2)}) async-start(f32[128,1728,1,2]{1,3,2,0:T(2,128)} %bitcast.62), calls=%async_computation.5 | async-start | bytes 3670016 | tf_op jit(solution)/shard_map/all_to_all | solution.py:51
  833.6 24.3 %all-to-all-done.5 = f32[128,1728,1,2]{1,3,2,0:T(2,128)S(1)} async-done(((f32[128,1728,1,2]{1,3,2,0:T(2,128)}), f32[128,1728,1,2]{1,3,2,0:T(2,128)S(1)}, u32[]{:S(2)}, u32[]{:S(2)}) %all-to-all-start.5) | async-done | bytes 1769504 | tf_op jit(solution)/shard_map/all_to_all | solution.py:51
  860.4 6.6 scatter_custom_fusion.8
  867.0 5.1 copy.116
  (143 shorter events, 123.5 us)
Async XLA Ops:
  0.6 351.1 %copy-start = (bf16[256,256]{1,0:T(8,128)(2,1)S(1)}, bf16[256,256]{1,0:T(8,128)(2,1)}, u32[]{:S(2)}) copy-start(bf16[256,256]{1,0:T(8,128)(2,1)} %param.30) | copy-start | bytes 393220
  1.5 40.4 %collective-permute-start = (f32[54,1,2,128]{3,2,1,0:T(2,128)S(1)}, f32[54,1,2,128]{3,2,1,0:T(2,128)S(1)}, u32[]{:S(2)}, u32[]{:S(2)}) collective-permute-start(f32[54,1,2,128]{3,2,1,0:T(2,128)S(1)} %get-tuple-element.25), channel_id=1, source_target_pairs={{0,32},{32,64},{64,96},{1,33},{33,65},{65,97},{2,34},{34,66},{66,9... | collective-permute-start | bytes 165896 | tf_op jit(solution)/shard_map/ppermute | solution.py:21
  6.6 36.3 %collective-permute-start.3 = (f32[54,2,1,128]{3,2,1,0:T(1,128)S(1)}, f32[54,2,1,128]{3,2,1,0:T(1,128)S(1)}, u32[]{:S(2)}, u32[]{:S(2)}) collective-permute-start(f32[54,2,1,128]{3,2,1,0:T(1,128)S(1)} %get-tuple-element.23), channel_id=1, source_target_pairs={{1,0},{2,1},{3,2},{4,3},{5,4},{6,5},{7,6},{8,7},{9,8},{10,9},{11,1... | collective-permute-start | bytes 165896 | tf_op jit(solution)/shard_map/ppermute | solution.py:22
  9.4 33.4 %collective-permute-start.1 = (f32[54,1,2,128]{3,2,1,0:T(2,128)S(1)}, f32[54,1,2,128]{3,2,1,0:T(2,128)S(1)}, u32[]{:S(2)}, u32[]{:S(2)}) collective-permute-start(f32[54,1,2,128]{3,2,1,0:T(2,128)S(1)} %get-tuple-element.24), channel_id=1, source_target_pairs={{32,0},{64,32},{96,64},{33,1},{65,33},{97,65},{34,2},{66,34},{98,6... | collective-permute-start | bytes 165896 | tf_op jit(solution)/shard_map/ppermute | solution.py:22
  10.7 32.2 %collective-permute-start.2 = (f32[54,2,1,128]{3,2,1,0:T(1,128)S(1)}, f32[54,2,1,128]{3,2,1,0:T(1,128)S(1)}, u32[]{:S(2)}, u32[]{:S(2)}) collective-permute-start(f32[54,2,1,128]{3,2,1,0:T(1,128)S(1)} %get-tuple-element.22), channel_id=1, source_target_pairs={{0,1},{1,2},{2,3},{3,4},{4,5},{5,6},{6,7},{7,8},{8,9},{9,10},{10,1... | collective-permute-start | bytes 165896 | tf_op jit(solution)/shard_map/ppermute | solution.py:21
  16.7 52.6 %copy-start.1 = (f32[512]{0:T(512)S(1)}, f32[512]{0:T(512)}, u32[]{:S(2)}) copy-start(f32[512]{0:T(512)} %param.27) | copy-start | bytes 6148
  21.1 19.6 %all-to-all-start = ((s32[1,32,24]{2,0,1:T(1,128)}), s32[1,32,24]{2,0,1:T(1,128)S(1)}, u32[]{:S(2)}, u32[]{:S(2)}) async-start(s32[1,32,24]{2,0,1:T(1,128)} %bitcast.7), calls=%async_computation | async-start | bytes 32768 | tf_op jit(solution)/shard_map/all_to_all | solution.py:144
  47.5 15.6 %all-to-all-start.1 = ((f32[32,1,1296]{2,1,0:T(1,128)}), f32[32,1,1296]{2,1,0:T(1,128)S(1)}, u32[]{:S(2)}, u32[]{:S(2)}) async-start(f32[32,1,1296]{2,1,0:T(1,128)} %reshape.539), calls=%async_computation.1 | async-start | bytes 360448 | tf_op jit(solution)/shard_map/all_to_all | solution.py:143
  344.3 3.4 copy-start.5
  347.7 4.1 copy-start.6
  361.4 12.5 %copy-start.3 = (s32[1,256]{1,0:T(1,128)S(1)}, s32[1,256]{1,0:T(1,128)}, u32[]{:S(2)}) copy-start(s32[1,256]{1,0:T(1,128)} %param.34) | copy-start | bytes 3076
  365.9 31.6 %copy-start.2 = (f32[2,2,128]{2,1,0:T(2,128)S(1)}, f32[2,2,128]{2,1,0:T(2,128)}, u32[]{:S(2)}) copy-start(f32[2,2,128]{2,1,0:T(2,128)} %param.23) | copy-start | bytes 6148
  370.0 12.2 %all-to-all-start.2 = ((f32[32,1,1296]{2,1,0:T(1,128)}), f32[32,1,1296]{2,1,0:T(1,128)S(1)}, u32[]{:S(2)}, u32[]{:S(2)}) async-start(f32[32,1,1296]{2,1,0:T(1,128)} %reshape.541), calls=%async_computation.2 | async-start | bytes 360448 | tf_op jit(solution)/shard_map/all_to_all | solution.py:164
  385.2 11.4 %collective-permute-start.4 = (f32[54,1,2,128]{3,2,1,0:T(2,128)S(1)}, f32[54,1,2,128]{3,2,1,0:T(2,128)S(1)}, u32[]{:S(2)}, u32[]{:S(2)}) collective-permute-start(f32[54,1,2,128]{3,2,1,0:T(2,128)S(1)} %get-tuple-element.17), channel_id=1, source_target_pairs={{0,32},{32,64},{64,96},{1,33},{33,65},{65,97},{2,34},{34,66},{66,9... | collective-permute-start | bytes 165896 | tf_op jit(solution)/shard_map/ppermute | solution.py:21
  389.5 7.1 collective-permute-start.7
  392.0 5.5 collective-permute-start.5
  393.3 4.3 collective-permute-start.6
  401.1 49.0 %all-to-all-start.3 = ((f32[32,1,1296]{2,1,0:T(1,128)}), f32[32,1,1296]{2,1,0:T(1,128)S(1)}, u32[]{:S(2)}, u32[]{:S(2)}) async-start(f32[32,1,1296]{2,1,0:T(1,128)} %reshape.543), calls=%async_computation.3 | async-start | bytes 360448 | tf_op jit(solution)/shard_map/all_to_all | solution.py:143
  756.8 63.1 %all-to-all-start.4 = ((f32[32,1,1296]{2,1,0:T(1,128)}), f32[32,1,1296]{2,1,0:T(1,128)S(1)}, u32[]{:S(2)}, u32[]{:S(2)}) async-start(f32[32,1,1296]{2,1,0:T(1,128)} %reshape.545), calls=%async_computation.4 | async-start | bytes 360448 | tf_op jit(solution)/shard_map/all_to_all | solution.py:164
  817.5 12.7 %copy-start.4 = (s32[1,256]{1,0:T(1,128)S(1)}, s32[1,256]{1,0:T(1,128)}, u32[]{:S(2)}) copy-start(s32[1,256]{1,0:T(1,128)} %param.35) | copy-start | bytes 3076
  819.9 38.1 %all-to-all-start.5 = ((f32[128,1728,1,2]{1,3,2,0:T(2,128)}), f32[128,1728,1,2]{1,3,2,0:T(2,128)S(1)}, u32[]{:S(2)}, u32[]{:S(2)}) async-start(f32[128,1728,1,2]{1,3,2,0:T(2,128)} %bitcast.62), calls=%async_computation.5 | async-start | bytes 3670016 | tf_op jit(solution)/shard_map/all_to_all | solution.py:51
where the time goes:
time: 884 us; the launch traced here: 872 us
  local copies, waits for them, and re-layouts  623 us (70%)
  other arithmetic  120 us (14%)
  starting transfers between devices  68.9 us (8%)
  waiting for transfers between devices  41 us (5%)
  matrix products  17 us (2%)
    gather x4, local copies, waits for them, and re-layouts, particle_section(): partner_state = jnp.take_along_axis(state, partner[None, :, :], axis=1)  488 us
    scatter-add x2, other arithmetic, particle_section(): state = state.at[:, :, chosen_slots].add(change)  68 us
    all_to_all x1, waiting for transfers between devices, one_exchange(): lax.all_to_all(blocks, axis, split_axis=0, concat_axis=0, tiled=True)  24.3 us
    add x2, local copies, waits for them, and re-layouts, particle_section(): state = state + PAIR_WEIGHT * (partner_state - state)  18.1 us
  transfers between devices with their start and end apart: 14, of which 5 were waited for; matrix products, arithmetic and copies ran while one was open for 14% of the time, Pallas kernels for 0%

commit v1 on v0

v1 whole, which is shorter than its diff:
```python
import functools

import jax
import jax.numpy as jnp
from jax import lax
from jax.experimental import pallas as pl
from jax.experimental.pallas import tpu as pltpu
from jax.sharding import PartitionSpec as P

F32, BF16 = jnp.float32, jnp.bfloat16
MESH = pl.DeviceIdType.MESH

NS, NP, CELLS = 54, 32, 512
ROWS = NS * NP
OWNERS, GROUPS = 32, 4
HALF = 16
PLACES = 2 * OWNERS * HALF
LIST = 256
LABEL = 54
VMEM_LIMIT = 56 * 1024 * 1024
NT = (((1,), (1,)), ((), ()))


def split(x):
    hi = x.astype(BF16)
    return hi, (x - hi.astype(F32)).astype(BF16)


def mat(a, b):
    return jnp.dot(a, b, preferred_element_type=F32)


def mat_nt(a, b):
    return lax.dot_general(a, b, NT, preferred_element_type=F32)


def silu(a):
    h = 0.5 * a
    return (h + h * jnp.tanh(h)).astype(BF16)


def packed(picker, values):
    hi, lo = split(values)
    both = mat_nt(picker, jnp.concatenate([hi, lo], axis=0))
    both = both + pltpu.roll(both, 64, axis=1)
    lane = lax.broadcasted_iota(jnp.int32, (PLACES // 2, 128), 1)
    return jnp.where(lane < 64, both[: PLACES // 2], both[PLACES // 2 :])


def unpacked(message, placer):
    turned = message.T
    values = jnp.concatenate([turned[:64], turned[64:]], axis=1)
    hi, lo = split(values)
    both = mat(jnp.concatenate([hi, lo], axis=0), placer)
    return both[:64] + both[64:]


def step_kernel(
    grid_in, speed, parts_in, owner, slot, rate, partner, w_in, w_hid, w_out, listed, count, leave,
    grid_out, parts_out, moving,
    state, faces, halo, f_send, f_recv, s_send, s_recv, to_box, to_slot, reacting, feed, r_f, wi, wo,
    load_sem, store_sem, halo_send, halo_recv, fs_sem, fr_sem, ss_sem, sr_sem,
):
    gx, gy = lax.axis_index("gx"), lax.axis_index("gy")
    barrier = pltpu.get_barrier_semaphore()

    loads = [
        pltpu.make_async_copy(parts_in.at[:, pl.ds(128 * lb, 128)], state.at[lb], load_sem.at[lb]) for lb in range(4)
    ]
    stores = [
        pltpu.make_async_copy(state.at[lb], parts_out.at[:, pl.ds(128 * lb, 128)], store_sem.at[lb]) for lb in range(4)
    ]
    for copy in loads:
        copy.start()

    def greet(k, carry):
        pl.semaphore_signal(barrier, inc=1, device_id={"gy": lax.rem(gy + k, OWNERS)}, device_id_type=MESH)
        return carry

    lax.fori_loop(1, OWNERS, greet, 0)
    for d in (1, GROUPS - 1):
        pl.semaphore_signal(barrier, inc=1, device_id={"gx": lax.rem(gx + d, GROUPS)}, device_id_type=MESH)

    for q in range(4):
        faces[0, q // 2, q % 2, 0:NS, :] = grid_in[pl.ds(q, NS, stride=4), :]
        faces[0, q // 2, q % 2, NS:56, :] = jnp.zeros((56 - NS, 128), F32)

    pl.semaphore_wait(barrier, OWNERS - 1 + 2)

    def halo_copies(t):
        ahead = [
            (faces.at[t, 1], {"gx": lax.rem(gx + 1, GROUPS)}),
            (faces.at[t, 0], {"gx": lax.rem(gx + GROUPS - 1, GROUPS)}),
            (faces.at[t, :, 1], {"gy": lax.rem(gy + 1, OWNERS)}),
            (faces.at[t, :, 0], {"gy": lax.rem(gy + OWNERS - 1, OWNERS)}),
        ]
        return [
            pltpu.make_async_remote_copy(
                src_ref=source,
                dst_ref=halo.at[t, i],
                send_sem=halo_send.at[t, i],
                recv_sem=halo_recv.at[t, i],
                device_id=device,
                device_id_type=MESH,
            )
            for i, (source, device) in enumerate(ahead)
        ]

    def exchange(out, into, t, send_sem, recv_sem):
        def send(k, carry):
            other = lax.rem(gy + k, OWNERS)
            pltpu.make_async_remote_copy(
                src_ref=out.at[t, other],
                dst_ref=into.at[t, gy],
                send_sem=send_sem.at[t],
                recv_sem=recv_sem.at[t],
                device_id={"gy": other},
                device_id_type=MESH,
            ).start()
            return carry

        lax.fori_loop(1, OWNERS, send, 0)
        into[t, gy] = out[t, gy]

    def await_all(buf, t, sem):
        part = buf.at[t, pl.ds(0, OWNERS - 1)]
        pltpu.make_async_copy(part, part, sem.at[t]).wait()

    halos = [halo_copies(t) for t in range(2)]
    for copy in halos[0]:
        copy.start()

    owner_row = jnp.concatenate([owner[q : q + 1, :] for q in range(4)], axis=1)
    label_row = jnp.concatenate([slot[q : q + 1, :] for q in range(4)], axis=1).astype(F32) + 1.0
    mine = (lax.broadcasted_iota(jnp.int32, (OWNERS, CELLS), 0) == owner_row).astype(F32)
    before = (
        lax.broadcasted_iota(jnp.int32, (CELLS, CELLS), 0) < lax.broadcasted_iota(jnp.int32, (CELLS, CELLS), 1)
    ).astype(F32)
    ahead = mat(mine.astype(BF16), before.astype(BF16))
    rank = jnp.sum(mine * ahead, axis=0, keepdims=True)
    place = owner_row.astype(F32) * HALF + rank + jnp.where(rank >= HALF, float(PLACES // 2 - HALF), 0.0)
    place = place.astype(jnp.int32)
    to_box[...] = (lax.broadcasted_iota(jnp.int32, (PLACES, CELLS), 0) == place).astype(F32).astype(BF16)
    live = lax.broadcasted_iota(jnp.int32, (1, LIST), 1) < count[...]
    react_row = jnp.where(live, listed[...], CELLS)
    reacting[...] = (lax.broadcasted_iota(jnp.int32, (CELLS, LIST), 0) == react_row).astype(F32).astype(BF16)
    wi[...] = jnp.zeros_like(wi)
    wi[:, 0:NS] = w_in[...].astype(F32)
    wo[...] = jnp.zeros_like(wo)
    wo[0:NS, :] = w_out[...].astype(F32)
    feed[...] = jnp.zeros_like(feed)

    def mix():
        for lb in range(4):
            cols = slice(128 * lb, 128 * lb + 128)
            mates = [partner[8 * o : 8 * o + 8, cols] for o in range(4)]
            index = [m & 7 for m in mates]
            group = [m >> 3 for m in mates]

            def body(s, carry):
                base = pl.multiple_of(s * NP, NP)
                tiles = [state[lb, pl.ds(base + 8 * g, 8), :] for g in range(4)]
                for o in range(4):
                    mate = jnp.take_along_axis(tiles[0], index[o], axis=0, mode="promise_in_bounds")
                    for g in range(1, 4):
                        other = jnp.take_along_axis(tiles[g], index[o], axis=0, mode="promise_in_bounds")
                        mate = jnp.where(group[o] == g, other, mate)
                    state[lb, pl.ds(base + 8 * o, 8), :] = 0.6 * tiles[o] + 0.4 * mate
                return carry

            lax.fori_loop(0, NS, body, 0)

    def transport(t):
        x_low = jnp.where(gx > 0, 1.0, 0.0).astype(F32)
        x_high = jnp.where(gx < GROUPS - 1, 1.0, 0.0).astype(F32)
        y_low = jnp.where(gy > 0, 1.0, 0.0).astype(F32)
        y_high = jnp.where(gy < OWNERS - 1, 1.0, 0.0).astype(F32)
        made = []
        for x in range(2):
            for y in range(2):
                center = faces[t, x, y]
                up = faces[t, 0, y] if x else halo[t, 0, y] * x_low
                down = halo[t, 1, y] * x_high if x else faces[t, 1, y]
                left = faces[t, x, 0] if y else halo[t, 2, x] * y_low
                right = halo[t, 3, x] * y_high if y else faces[t, x, 1]
                around = up + down + left + right
                around = around + pltpu.roll(center, 1, axis=1) + pltpu.roll(center, 127, axis=1)
                q = 2 * x + y
                made.append(center + 0.1 * (around - 6.0 * center) - speed[q : q + 1, :] * (center - up))
        return jnp.concatenate(made, axis=1)

    rate_row = rate[...]
    keep_row = 1.0 - rate_row

    def chemistry(t):
        weights_in = wi[...].astype(BF16)
        weights_hid = w_hid[...]
        weights_out = wo[...].astype(BF16)

        def body(g, total):
            for i in range(4):
                own = jnp.concatenate(
                    [state[lb, pl.ds(4 * g + i, NS, stride=NP), :] for lb in range(4)], axis=1
                )
                feed[64 * i : 64 * i + NS, :] = own * keep_row + r_f[0:NS, :]
            chosen = mat(feed[...].astype(BF16), reacting[...]).astype(BF16)
            columns = jnp.concatenate([chosen[64 * i : 64 * i + 64] for i in range(4)], axis=1)
            one = silu(mat(weights_in, columns))
            two = silu(mat(weights_hid, one))
            change = mat(weights_out, two).astype(BF16)
            parts = [change[:, LIST * i : LIST * i + LIST] for i in range(4)]
            back = mat_nt(jnp.concatenate(parts, axis=0), reacting[...])
            for i in range(4):
                made = feed[64 * i : 64 * i + NS, :] + back[64 * i : 64 * i + NS, :]
                for lb in range(4):
                    state[lb, pl.ds(4 * g + i, NS, stride=NP), :] = made[:, 128 * lb : 128 * lb + 128]
                total = total + parts[i].astype(F32)
            return total

        total = lax.fori_loop(0, NP // 4, body, jnp.zeros((64, LIST), F32))
        hi, lo = split(total * (1.0 / NP))
        both = mat_nt(jnp.concatenate([hi, lo], axis=0), reacting[...])
        return both[:64] + both[64:]

    row = lax.broadcasted_iota(jnp.int32, (64, CELLS), 0)
    for t in range(2):
        for copy in halos[t]:
            copy.wait_recv()
        grid = jnp.concatenate([transport(t), jnp.zeros((8, CELLS), F32)], axis=0)
        message = packed(to_box[...], jnp.where(row == LABEL, label_row, grid))
        for j in range(OWNERS):
            f_send[t, j] = message[HALF * j : HALF * j + HALF]
        exchange(f_send, f_recv, t, fs_sem, fr_sem)
        if t == 0:
            for copy in loads:
                copy.wait()
        mix()
        await_all(f_recv, t, fr_sem)
        arrived = f_recv[t].reshape(PLACES // 2, 128)
        if t == 0:
            lane = lax.broadcasted_iota(jnp.int32, (PLACES // 2, CELLS), 1).astype(F32) + 1.0
            for h in range(2):
                labels = arrived[:, 64 * h + LABEL : 64 * h + LABEL + 1]
                to_slot[h * PLACES // 2 : (h + 1) * PLACES // 2, :] = (labels == lane).astype(F32).astype(BF16)
        r_f[...] = unpacked(arrived, to_slot[...]) * rate_row
        source = chemistry(t)
        message = packed(to_slot[...], source)
        for j in range(OWNERS):
            s_send[t, j] = message[HALF * j : HALF * j + HALF]
        exchange(s_send, s_recv, t, ss_sem, sr_sem)
        if t == 1:
            for copy in stores:
                copy.start()
            goes = (lax.broadcasted_iota(jnp.int32, (CELLS, LIST), 0) == leave[...]).astype(F32)
            goes = goes.T.astype(BF16)
            for j in range(14):
                size = min(128, ROWS - 128 * j)
                block = [state[lb, 128 * j : 128 * j + size, :] for lb in range(4)]
                hi, lo = split(jnp.concatenate(block, axis=1))
                moving[:, j, 0:size] = mat_nt(goes, hi) + mat_nt(goes, lo)
            moving[:, 13, 64:128] = jnp.zeros((LIST, 64), F32)
        await_all(s_recv, t, sr_sem)
        grid = grid + unpacked(s_recv[t].reshape(PLACES // 2, 128), to_box[...])
        if t == 0:
            for q in range(4):
                faces[1, q // 2, q % 2] = grid[0:56, 128 * q : 128 * q + 128]
            for copy in halos[1]:
                copy.start()
        else:
            for q in range(4):
                grid_out[pl.ds(q, NS, stride=4), :] = grid[0:NS, 128 * q : 128 * q + 128]
    for copy in stores:
        copy.wait()
    for t in range(2):
        for copy in halos[t]:
            copy.wait_send()
        await_all(f_send, t, fs_sem)
        await_all(s_send, t, ss_sem)


def settle_kernel(parts_in, arrived, arrive, parts_out, state, load_sem, store_sem):
    def span(j):
        return pl.ds(128 * j, min(128, ROWS - 128 * j))

    loads = [pltpu.make_async_copy(parts_in.at[span(j)], state.at[span(j)], load_sem.at[j]) for j in range(14)]
    stores = [pltpu.make_async_copy(state.at[span(j)], parts_out.at[span(j)], store_sem.at[j]) for j in range(14)]
    for copy in loads:
        copy.start()
    lands = (lax.broadcasted_iota(jnp.int32, (CELLS, LIST), 0) == arrive[...]).astype(F32).astype(BF16)
    taken = mat_nt(jnp.ones((8, LIST), BF16), lands)[0:1]
    for j in range(14):
        size = min(128, ROWS - 128 * j)
        hi, lo = split(arrived[:, j, :].T)
        moved = mat_nt(hi, lands) + mat_nt(lo, lands)
        loads[j].wait()
        kept = state[128 * j : 128 * j + size, :]
        state[128 * j : 128 * j + size, :] = jnp.where(taken > 0.5, moved[0:size], kept)
        stores[j].start()
    for copy in stores:
        copy.wait()


def per_device(
    grid_scalars, axial_speed, particles, cell_owner, cell_slot, mix_rate, partner,
    chem_input, chem_hidden, chem_output, react_slots, react_count, leave_slots, arrive_slots,
):
    vmem = pl.BlockSpec(memory_space=pltpu.VMEM)
    hbm = pl.BlockSpec(memory_space=pl.ANY)
    dma = pltpu.SemaphoreType.DMA
    messages = pltpu.VMEM((2, OWNERS, HALF, 128), F32)
    grid, parts, moving = pl.pallas_call(
        step_kernel,
        out_shape=(
            jax.ShapeDtypeStruct((4 * NS, 128), F32),
            jax.ShapeDtypeStruct((ROWS, CELLS), F32),
            jax.ShapeDtypeStruct((LIST, 14, 128), F32),
        ),
        in_specs=[vmem, vmem, hbm] + [vmem] * 10,
        out_specs=(vmem, hbm, vmem),
        scratch_shapes=[
            pltpu.VMEM((4, ROWS, 128), F32),
            pltpu.VMEM((2, 2, 2, 56, 128), F32),
            pltpu.VMEM((2, 4, 2, 56, 128), F32),
            messages,
            messages,
            messages,
            messages,
            pltpu.VMEM((PLACES, CELLS), BF16),
            pltpu.VMEM((PLACES, CELLS), BF16),
            pltpu.VMEM((CELLS, LIST), BF16),
            pltpu.VMEM((256, CELLS), F32),
            pltpu.VMEM((64, CELLS), F32),
            pltpu.VMEM((256, 64), F32),
            pltpu.VMEM((64, 256), F32),
            dma((4,)),
            dma((4,)),
            dma((2, 4)),
            dma((2, 4)),
            dma((2,)),
            dma((2,)),
            dma((2,)),
            dma((2,)),
        ],
        compiler_params=pltpu.CompilerParams(
            collective_id=0, has_side_effects=True, vmem_limit_bytes=VMEM_LIMIT
        ),
        name="step",
    )(
        grid_scalars.reshape(4 * NS, 128),
        axial_speed.reshape(4, 128),
        particles.reshape(ROWS, CELLS),
        cell_owner.reshape(4, 128),
        cell_slot.reshape(4, 128),
        mix_rate.reshape(1, CELLS),
        partner,
        chem_input,
        chem_hidden,
        chem_output,
        react_slots,
        react_count.reshape(1, 1),
        leave_slots,
    )
    arrived = lax.all_to_all(moving.reshape(128, 2, 14, 128), ("gx", "gy"), 0, 0, tiled=True)
    out = pl.pallas_call(
        settle_kernel,
        out_shape=jax.ShapeDtypeStruct((ROWS, CELLS), F32),
        in_specs=[hbm, vmem, vmem],
        out_specs=hbm,
        scratch_shapes=[pltpu.VMEM((ROWS, CELLS), F32), dma((14,)), dma((14,))],
        compiler_params=pltpu.CompilerParams(vmem_limit_bytes=VMEM_LIMIT),
        name="settle",
    )(parts, arrived.reshape(LIST, 14, 128), arrive_slots)
    return grid.reshape(grid_scalars.shape), out.reshape(particles.shape)


def solution(mesh):
    placed = (
        P(None, "gx", "gy", None),
        P("gx", "gy", None),
        P(None, None, ("gx", "gy")),
        P("gx", "gy", None),
        P("gx", "gy", None),
        P(("gx", "gy")),
        P(None, ("gx", "gy")),
        P(),
        P(),
        P(),
        P(("gx", "gy"), None),
        P(("gx", "gy")),
        P(("gx", "gy"), None),
        P(("gx", "gy"), None),
    )
    return jax.shard_map(
        per_device,
        mesh=mesh,
        in_specs=placed,
        out_specs=(P(None, "gx", "gy", None), P(None, None, ("gx", "gy"))),
        check_vma=False,
    )
```

time: 884 us -> 128 us (0.14); the launches traced: 872 us -> 128 us
  local copies, waits for them, and re-layouts: 623 us -> 7.59 us
  other arithmetic: 120 us -> 0 us
  Pallas kernels: 0 us -> 85.6 us
  starting transfers between devices: 68.9 us -> 5.78 us
  matrix products: 17 us -> 0 us
  waiting for transfers between devices: 41 us -> 27.7 us
    gather x15 -> x0, local copies, waits for them, and re-layouts: 515 us -> none  [the longest x4 488 us: particle_section(): partner_state = jnp.take_along_axis(state, partner[None, :, :], axis=1)]
    pallas_call x0 -> x2, Pallas kernels: none -> 85.6 us  [the longest x1 77.1 us: per_device(): pl.pallas_call(step_kernel, out_shape=(jax.ShapeDtypeStruct((4 * NS, 128)...]
    scatter-add x2 -> x0, other arithmetic: 68 us -> none  [particle_section(): state = state.at[:, :, chosen_slots].add(change)]
    all_to_all x6 -> x1, starting transfers between devices: 46.2 us -> 5.78 us  [per_device(): lax.all_to_all(moving.reshape(128, 2, 14, 128), ('gx', 'gy'), 0, 0, tiled...]
    add x4 -> x0, local copies, waits for them, and re-layouts: 32.1 us -> none  [the longest x2 18.1 us: particle_section(): state = state + PAIR_WEIGHT * (partner_state - state)]
    scatter x8 -> x0, local copies, waits for them, and re-layouts: 25.6 us -> none  [the longest x2 11.6 us: per_device(): flat_parts.at[:, arrive_slots[0]].set(arrived_cells, mode='drop')]
    ppermute x8 -> x0, starting transfers between devices: 22.7 us -> none  [the longest x4 14.7 us: with_halo(): lax.ppermute(last, axis, up)]
    add x6 -> x0, other arithmetic: 22.4 us -> none  [the longest x2 12.4 us: particle_section(): state = state + PAIR_WEIGHT * (partner_state - state)]
  transfers between devices with their start and end apart: 14 -> 1, of which waited for: 5 -> 1; matrix products, arithmetic and copies ran while one was open for 14% -> 0% of each run, Pallas kernels for 0% -> 0%
where the time goes in v1:
time: 128 us
  Pallas kernels  85.6 us (67%)
  waiting for transfers between devices  27.7 us (22%)
  local copies, waits for them, and re-layouts  7.59 us (6%)
  starting transfers between devices  5.78 us (5%)
  between operations  1.31 us (1%)
    pallas_call x1, Pallas kernels, per_device(): pl.pallas_call(step_kernel, out_shape=(jax.ShapeDtypeStruct((4 * NS, 128)...  77.1 us
    all_to_all x1, waiting for transfers between devices, per_device(): lax.all_to_all(moving.reshape(128, 2, 14, 128), ('gx', 'gy'), 0, 0, tiled...  27.7 us
    pallas_call x1, Pallas kernels, per_device(): pl.pallas_call(settle_kernel, out_shape=jax.ShapeDtypeStruct((ROWS, CELLS...  8.44 us
    all_to_all x1, starting transfers between devices, per_device(): lax.all_to_all(moving.reshape(128, 2, 14, 128), ('gx', 'gy'), 0, 0, tiled...  5.78 us
    reshape x1, local copies, waits for them, and re-layouts, per_device(): moving.reshape(128, 2, 14, 128)  3.76 us
  transfers between devices with their start and end apart: 1, of which 1 were waited for; matrix products, arithmetic and copies ran while one was open for 0% of the time, Pallas kernels for 0%

profile of v1, /device:TPU:1, one launch (start us, length us, event | category | flops | bytes accessed | tf_op | source)
XLA Modules:
  0.0 128.0 jit_solution(4458565331562353488)
XLA Ops:
  1.3 1.5 %copy.17.w_in = bf16[256,54]{1,0:T(8,128)(2,1)} copy(bf16[256,54]{0,1:T(8,128)(2,1)} %param.21) | data formatting | bytes 55296 | tf_op args[7]
  2.8 77.1 %step.1 = (f32[216,128]{1,0:T(8,128)}, f32[1728,512]{1,0:T(8,128)}, f32[256,14,128]{2,1,0:T(8,128)}) custom-call(f32[216,128]{1,0:T(8,128)} %bitcast.17, f32[4,128]{1,0:T(4,128)} %bitcast.18, f32[1728,512]{1,0:T(8,128)} %bitcast.14, s32[4,128]{1,0:T(4,128)} %bitcast.19, s32[4,128]{1,0:T(4,128)} %bitcast.20, f32[1,512]{1,0:T(1,128)} %bitcast.21, ...), custom_call_target="tpu_custom_call" | custom-call | tf_op jit(solution)/shard_map/step/pallas_call | solution.py:311
  79.9 3.8 %copy.18 = f32[128,2,14,128]{3,1,2,0:T(2,128)} copy(f32[128,2,14,128]{3,2,1,0:T(8,128)} %bitcast.15) | data formatting | bytes 3670016 | tf_op jit(solution)/shard_map/reshape | solution.py:363
  83.7 5.8 %all-to-all-start = ((f32[128,2,14,128]{3,1,2,0:T(2,128)}), f32[128,2,14,128]{3,1,2,0:T(2,128)S(1)}, u32[]{:S(2)}, u32[]{:S(2)}) async-start(f32[128,2,14,128]{3,1,2,0:T(2,128)} %copy.18), calls=%async_computation | async-start | bytes 3670016 | tf_op jit(solution)/shard_map/all_to_all | solution.py:363
  89.5 27.7 %all-to-all-done = f32[128,2,14,128]{3,1,2,0:T(2,128)S(1)} async-done(((f32[128,2,14,128]{3,1,2,0:T(2,128)}), f32[128,2,14,128]{3,1,2,0:T(2,128)S(1)}, u32[]{:S(2)}, u32[]{:S(2)}) %all-to-all-start) | async-done | bytes 1835040 | tf_op jit(solution)/shard_map/all_to_all | solution.py:363
  117.2 1.7 %copy.19 = f32[128,2,14,128]{3,2,1,0:T(8,128)} copy(f32[128,2,14,128]{3,1,2,0:T(2,128)S(1)} %all-to-all-done) | data formatting | bytes 3670016 | tf_op jit(solution)/shard_map/all_to_all | solution.py:363
  118.9 0.0 copy-start
  118.9 8.4 %settle.1 = f32[1728,512]{1,0:T(8,128)} custom-call(f32[1728,512]{1,0:T(8,128)} %get-tuple-element.6.parts_in, f32[256,14,128]{2,1,0:T(8,128)} %bitcast.12, s32[1,256]{1,0:T(1,128)} %arrive.1), custom_call_target="tpu_custom_call" | custom-call | tf_op jit(solution)/shard_map/settle/pallas_call | solution.py:364
  127.3 0.0 copy-done
  127.3 0.6 copy.22
Async XLA Ops:
  83.7 33.5 %all-to-all-start = ((f32[128,2,14,128]{3,1,2,0:T(2,128)}), f32[128,2,14,128]{3,1,2,0:T(2,128)S(1)}, u32[]{:S(2)}, u32[]{:S(2)}) async-start(f32[128,2,14,128]{3,1,2,0:T(2,128)} %copy.18), calls=%async_computation | async-start | bytes 3670016 | tf_op jit(solution)/shard_map/all_to_all | solution.py:363
  118.9 8.4 %copy-start = (f32[216,128]{1,0:T(8,128)S(1)}, f32[216,128]{1,0:T(8,128)}, u32[]{:S(2)}) copy-start(f32[216,128]{1,0:T(8,128)} %get-tuple-element.5) | copy-start | bytes 331780

commit v2 on v1

v2 whole, which is shorter than its diff:
```python
import functools

import jax
import jax.numpy as jnp
from jax import lax
from jax.experimental import pallas as pl
from jax.experimental.pallas import tpu as pltpu
from jax.sharding import PartitionSpec as P

F32, BF16 = jnp.float32, jnp.bfloat16
MESH = pl.DeviceIdType.MESH

NS, NP, CELLS = 54, 32, 512
ROWS = NS * NP
OWNERS, GROUPS, DEVICES = 32, 4, 128
HALF = 16
PLACES = 2 * OWNERS * HALF
LIST = 256
SPAN = 432
CHAINS, WIDE = 2, 4
LABEL = 54
VMEM_LIMIT = 56 * 1024 * 1024
NT = (((1,), (1,)), ((), ()))


def split(x):
    hi = x.astype(BF16)
    return hi, (x - hi.astype(F32)).astype(BF16)


def mat(a, b):
    return jnp.dot(a, b, preferred_element_type=F32)


def mat_nt(a, b):
    return lax.dot_general(a, b, NT, preferred_element_type=F32)


def silu(a):
    h = 0.5 * a
    return (h + h * jnp.tanh(h)).astype(BF16)


def packed(picker, values):
    hi, lo = split(values)
    both = mat_nt(picker, jnp.concatenate([hi, lo], axis=0))
    both = both + pltpu.roll(both, 64, axis=1)
    lane = lax.broadcasted_iota(jnp.int32, (PLACES // 2, 128), 1)
    return jnp.where(lane < 64, both[: PLACES // 2], both[PLACES // 2 :])


def unpacked(message, placer):
    turned = message.T
    values = jnp.concatenate([turned[:64], turned[64:]], axis=1)
    hi, lo = split(values)
    both = mat(jnp.concatenate([hi, lo], axis=0), placer)
    return both[:64] + both[64:]


def step_kernel(
    grid_in, speed, parts_in, owner, slot, rate, partner, w_in, w_hid, w_out, listed, count, leave, arrive,
    grid_out, parts_out,
    state, guest, faces, halo, f_send, f_recv, s_send, s_recv, moving, moved, r_moving, r_moved,
    to_box, to_slot, order, final, turn, mates, feed, r_f, r_late, r_g, made, wi, wo,
    load_sem, store_sem, halo_send, halo_recv, fs_sem, fr_sem, ss_sem, sr_sem, move_send, move_recv,
):
    gx, gy = lax.axis_index("gx"), lax.axis_index("gy")
    me = gx * OWNERS + gy
    barrier = pltpu.get_barrier_semaphore()

    loads = [
        pltpu.make_async_copy(parts_in.at[:, pl.ds(128 * lb, 128)], state.at[lb], load_sem.at[lb]) for lb in range(4)
    ]
    for copy in loads:
        copy.start()

    def device(k):
        other = lax.rem(me + k, DEVICES)
        return other, {"gx": other // OWNERS, "gy": lax.rem(other, OWNERS)}

    def greet(k, carry):
        pl.semaphore_signal(barrier, inc=1, device_id=device(k)[1], device_id_type=MESH)
        return carry

    lax.fori_loop(1, DEVICES, greet, 0)

    for q in range(4):
        faces[0, q // 2, q % 2, 0:NS, :] = grid_in[pl.ds(q, NS, stride=4), :]
        faces[0, q // 2, q % 2, NS:56, :] = jnp.zeros((56 - NS, 128), F32)

    pl.semaphore_wait(barrier, DEVICES - 1)

    def halo_copies(t):
        ahead = [
            (faces.at[t, 1], {"gx": lax.rem(gx + 1, GROUPS)}),
            (faces.at[t, 0], {"gx": lax.rem(gx + GROUPS - 1, GROUPS)}),
            (faces.at[t, :, 1], {"gy": lax.rem(gy + 1, OWNERS)}),
            (faces.at[t, :, 0], {"gy": lax.rem(gy + OWNERS - 1, OWNERS)}),
        ]
        return [
            pltpu.make_async_remote_copy(
                src_ref=source,
                dst_ref=halo.at[t, i],
                send_sem=halo_send.at[t, i],
                recv_sem=halo_recv.at[t, i],
                device_id=device,
                device_id_type=MESH,
            )
            for i, (source, device) in enumerate(ahead)
        ]

    def exchange(out, into, t, send_sem, recv_sem):
        def send(k, carry):
            other = lax.rem(gy + k, OWNERS)
            pltpu.make_async_remote_copy(
                src_ref=out.at[t, other],
                dst_ref=into.at[t, gy],
                send_sem=send_sem.at[t],
                recv_sem=recv_sem.at[t],
                device_id={"gy": other},
                device_id_type=MESH,
            ).start()
            return carry

        lax.fori_loop(1, OWNERS, send, 0)
        into[t, gy] = out[t, gy]

    def exchange_all(out, into, i):
        def send(k, carry):
            other, where = device(k)
            pltpu.make_async_remote_copy(
                src_ref=out.at[other],
                dst_ref=into.at[me],
                send_sem=move_send.at[i],
                recv_sem=move_recv.at[i],
                device_id=where,
                device_id_type=MESH,
            ).start()
            return carry

        lax.fori_loop(1, DEVICES, send, 0)
        into[me] = out[me]

    def await_all(part, sem):
        pltpu.make_async_copy(part, part, sem).wait()

    def await_row(buf, t, sem):
        await_all(buf.at[t, pl.ds(0, OWNERS - 1)], sem.at[t])

    halos = [halo_copies(t) for t in range(2)]
    for copy in halos[0]:
        copy.start()

    def iota(shape, dim):
        return lax.broadcasted_iota(jnp.int32, shape, dim)

    owner_row = jnp.concatenate([owner[q : q + 1, :] for q in range(4)], axis=1)
    label_row = jnp.concatenate([slot[q : q + 1, :] for q in range(4)], axis=1).astype(F32) + 1.0
    mine = (iota((OWNERS, CELLS), 0) == owner_row).astype(F32)
    before = (iota((CELLS, CELLS), 0) < iota((CELLS, CELLS), 1)).astype(F32)
    ahead = mat(mine.astype(BF16), before.astype(BF16))
    rank = jnp.sum(mine * ahead, axis=0, keepdims=True)
    place = owner_row.astype(F32) * HALF + rank + jnp.where(rank >= HALF, float(PLACES // 2 - HALF), 0.0)
    place = place.astype(jnp.int32)
    to_box[...] = (iota((PLACES, CELLS), 0) == place).astype(F32).astype(BF16)
    picks = (iota((CELLS, LIST), 0) == listed[...]).astype(F32)
    others = 1.0 - mat(picks.astype(BF16), jnp.ones((LIST, 128), BF16))
    later = (iota((CELLS, CELLS), 1) < iota((CELLS, CELLS), 0)).astype(F32)
    column = mat(later.astype(BF16), others.astype(BF16))
    column = jnp.where(others > 0.5, column, -1.0)[:, 0:1]
    rest = (column == iota((CELLS, LIST), 1).astype(F32)).astype(F32)
    chosen = jnp.concatenate([picks, rest], axis=1)
    order[...] = chosen.astype(BF16)
    live_row = (iota((1, LIST), 1) < count[...]).astype(F32)
    wi[...] = jnp.zeros_like(wi)
    wi[0:NS, :] = w_in[...].astype(F32)
    wo[...] = jnp.zeros_like(wo)
    wo[0:NS, :] = w_out[...].astype(F32)
    feed[...] = jnp.zeros_like(feed)
    weights_in = wi[...].T[:, 0:64].astype(BF16)
    weights_out = wo[...].astype(BF16)
    mates[0] = partner[...]

    def mix(t, keep_row):
        for lb in range(4):
            cols = slice(128 * lb, 128 * lb + 128)
            index = [mates[t, 8 * o : 8 * o + 8, cols] & 7 for o in range(4)]
            group = [mates[t, 8 * o : 8 * o + 8, cols] >> 3 for o in range(4)]
            late = t == 1 and lb >= 2

            def body(s, carry):
                base = pl.multiple_of(s * NP, NP)
                tiles = [state[lb, pl.ds(base + 8 * g, 8), :] for g in range(4)]
                for o in range(4):
                    mate = jnp.take_along_axis(tiles[0], index[o], axis=0, mode="promise_in_bounds")
                    for g in range(1, 4):
                        other = jnp.take_along_axis(tiles[g], index[o], axis=0, mode="promise_in_bounds")
                        mate = jnp.where(group[o] == g, other, mate)
                    mixed = 0.6 * tiles[o] + 0.4 * mate
                    if late:
                        mixed = mixed * keep_row[:, cols] + r_late[lb - 2, pl.ds(s, 1), :]
                    state[lb, pl.ds(base + 8 * o, 8), :] = mixed
                return carry

            lax.fori_loop(0, NS, body, 0, unroll=2)

    def rows_of(ref, blocks, start, size):
        return jnp.concatenate([ref[lb, start : start + size, :] for lb in range(blocks)], axis=1)

    def permute():
        for k in range(ROWS // SPAN):
            hi, lo = split(rows_of(state, 4, SPAN * k, SPAN))
            turned = mat(hi, order[...]) + mat(lo, order[...])
            for lb in range(4):
                state[lb, SPAN * k : SPAN * k + SPAN, :] = turned[:, 128 * lb : 128 * lb + 128]

    def transport(t):
        x_low = jnp.where(gx > 0, 1.0, 0.0).astype(F32)
        x_high = jnp.where(gx < GROUPS - 1, 1.0, 0.0).astype(F32)
        y_low = jnp.where(gy > 0, 1.0, 0.0).astype(F32)
        y_high = jnp.where(gy < OWNERS - 1, 1.0, 0.0).astype(F32)
        done = []
        for x in range(2):
            for y in range(2):
                center = faces[t, x, y]
                up = faces[t, 0, y] if x else halo[t, 0, y] * x_low
                down = halo[t, 1, y] * x_high if x else faces[t, 1, y]
                left = faces[t, x, 0] if y else halo[t, 2, x] * y_low
                right = halo[t, 3, x] * y_high if y else faces[t, x, 1]
                around = up + down + left + right
                around = around + pltpu.roll(center, 1, axis=1) + pltpu.roll(center, 127, axis=1)
                q = 2 * x + y
                done.append(center + 0.1 * (around - 6.0 * center) - speed[q : q + 1, :] * (center - up))
        return jnp.concatenate(done, axis=1)

    def chemistry(ref, keep, source, live):
        def body(g, total):
            for c in range(CHAINS):
                for i in range(WIDE):
                    p = (CHAINS * g + c) * WIDE + i
                    own = jnp.concatenate([ref[lb, pl.ds(p, NS, stride=NP), :] for lb in range(2)], axis=1)
                    feed[c * WIDE + i, 0:NS, :] = own * keep + source[0:NS, 0:LIST]
            columns = [
                jnp.concatenate(
                    [jnp.where(live > 0.5, feed[c * WIDE + i], 0.0).astype(BF16) for i in range(WIDE)], axis=1
                )
                for c in range(CHAINS)
            ]
            one = [silu(mat(weights_in, x)) for x in columns]
            two = [silu(mat(w_hid[...], x)) for x in one]
            change = [mat(weights_out, x).astype(BF16).astype(F32) for x in two]
            for c in range(CHAINS):
                for i in range(WIDE):
                    p = (CHAINS * g + c) * WIDE + i
                    part = jnp.where(live > 0.5, change[c][:, LIST * i : LIST * i + LIST], 0.0)
                    done = feed[c * WIDE + i] + part
                    for lb in range(2):
                        ref[lb, pl.ds(p, NS, stride=NP), :] = done[0:NS, 128 * lb : 128 * lb + 128]
                    total = total + part
            return total

        return lax.fori_loop(0, NP // (CHAINS * WIDE), body, jnp.zeros((64, LIST), F32))

    def through(values, matrix, product=mat):
        hi, lo = split(values)
        both = product(jnp.concatenate([hi, lo], axis=0), matrix)
        return both[: values.shape[0]] + both[values.shape[0] :]

    row = iota((64, CELLS), 0)
    for t in range(2):
        for copy in halos[t]:
            copy.wait_recv()
        grid = jnp.concatenate([transport(t), jnp.zeros((8, CELLS), F32)], axis=0)
        message = packed(to_box[...], jnp.where(row == LABEL, label_row, grid))
        for j in range(OWNERS):
            f_send[t, j] = message[HALF * j : HALF * j + HALF]
        exchange(f_send, f_recv, t, fs_sem, fr_sem)
        if t == 0:
            for copy in loads:
                copy.wait()
            mix(0, None)
            permute()
            mates[1] = mat(partner[...].astype(F32).astype(BF16), order[...]).astype(jnp.int32)
            rate_row = through(jnp.broadcast_to(rate[...], (8, CELLS)), order[...])[0:1]
            keep_row = 1.0 - rate_row
            goes = (iota((CELLS, LIST), 0) == leave[...]).astype(F32)
            goes = mat(goes.T.astype(BF16), order[...])
            for lb in range(4):
                turn[lb] = goes[:, 128 * lb : 128 * lb + 128]
            halves = [
                jnp.concatenate([turn[lb, pl.ds(c, DEVICES, stride=2), :] for lb in range(4)], axis=1) for c in range(2)
            ]
            goes_halves = jnp.concatenate(halves, axis=0).astype(BF16)
            goes = goes.astype(BF16)
            lands = (iota((CELLS, LIST), 0) == arrive[...]).astype(F32)
            taken = mat_nt(jnp.ones((8, LIST), BF16), lands.astype(BF16))[0:1]
            lands = lands.T
            for lb in range(4):
                turn[lb] = lands[:, 128 * lb : 128 * lb + 128]
            final[0:CELLS, :] = jnp.where(taken > 0.5, 0.0, chosen.T).astype(BF16)
            for c in range(2):
                final[CELLS + DEVICES * c : CELLS + DEVICES * (c + 1), :] = jnp.concatenate(
                    [turn[lb, pl.ds(c, DEVICES, stride=2), :] for lb in range(4)], axis=1
                ).astype(BF16)
        await_row(f_recv, t, fr_sem)
        arrived = f_recv[t].reshape(PLACES // 2, 128)
        if t == 0:
            lane = iota((PLACES // 2, CELLS), 1).astype(F32) + 1.0
            for h in range(2):
                labels = arrived[:, 64 * h + LABEL : 64 * h + LABEL + 1]
                to_slot[h * PLACES // 2 : (h + 1) * PLACES // 2, :] = (labels == lane).astype(F32).astype(BF16)
        r_f[...] = through(unpacked(arrived, to_slot[...]), order[...]) * rate_row
        for lb in range(2):
            r_late[lb] = r_f[:, LIST + 128 * lb : LIST + 128 * lb + 128]
        if t == 1:
            hi, lo = split(r_f[...])
            both = mat_nt(goes_halves, jnp.concatenate([hi, lo], axis=0))
            both = both + pltpu.roll(both, 64, axis=1)
            r_moving[:, 0, :] = jnp.where(iota((DEVICES, 128), 1) < 64, both[:DEVICES], both[DEVICES:])
            exchange_all(r_moving, r_moved, 1)
        total = chemistry(state, keep_row[:, 0:LIST], r_f, live_row)
        source = through(total * (1.0 / NP), order[:, 0:LIST], mat_nt)
        message = packed(to_slot[...], source)
        for j in range(OWNERS):
            s_send[t, j] = message[HALF * j : HALF * j + HALF]
        exchange(s_send, s_recv, t, ss_sem, sr_sem)
        if t == 0:
            mix(1, keep_row)
            for j in range(13):
                hi, lo = split(rows_of(state, 4, 128 * j, 128))
                value = mat_nt(goes, hi) + mat_nt(goes, lo)
                moving[:, :, j, :] = value.reshape(DEVICES, 2, 128)
            live_all = jnp.concatenate([live_row, jnp.zeros((1, LIST), F32)], axis=1)
            extra = jnp.where(row == 0, rate_row, jnp.where(row == 1, live_all, 0.0))
            hi, lo = split(jnp.concatenate([rows_of(state, 4, 1664, 64), extra], axis=0))
            value = mat_nt(goes, hi) + mat_nt(goes, lo)
            moving[:, :, 13, :] = value.reshape(DEVICES, 2, 128)
            exchange_all(moving, moved, 0)
        else:
            await_all(moved.at[pl.ds(0, DEVICES - 1)], move_recv.at[0])
            await_all(r_moved.at[pl.ds(0, DEVICES - 1)], move_recv.at[1])
            metas = []
            for c in range(2):
                for j in range(14):
                    block = moved[:, c, j, :].T
                    size = min(128, ROWS - 128 * j)
                    guest[c, 128 * j : 128 * j + size, :] = block[0:size]
                metas.append(block[64:72])
            metas = jnp.concatenate(metas, axis=1)
            r_turned = r_moved[...].reshape(DEVICES, 128).T
            r_g[...] = jnp.concatenate([r_turned[0:64], r_turned[64:128]], axis=1)
            chemistry(guest, 1.0 - metas[0:1], r_g, metas[1:2])

            def relax(s, carry):
                base = pl.multiple_of(s * NP, NP)
                for lb in range(2, 4):
                    cols = slice(128 * lb, 128 * lb + 128)
                    span = pl.ds(base, NP)
                    state[lb, span, :] = state[lb, span, :] * keep_row[:, cols] + r_late[lb - 2, pl.ds(s, 1), :]
                return carry

            lax.fori_loop(0, NS, relax, 0)
            stores = [
                pltpu.make_async_copy(
                    made.at[pl.ds(SPAN * k, SPAN)], parts_out.at[pl.ds(SPAN * k, SPAN)], store_sem.at[k]
                )
                for k in range(ROWS // SPAN)
            ]
            for k in range(ROWS // SPAN):
                block = [rows_of(state, 4, SPAN * k, SPAN), rows_of(guest, 2, SPAN * k, SPAN)]
                hi, lo = split(jnp.concatenate(block, axis=1))
                made[SPAN * k : SPAN * k + SPAN, :] = mat(hi, final[...]) + mat(lo, final[...])
                stores[k].start()
        await_row(s_recv, t, sr_sem)
        grid = grid + unpacked(s_recv[t].reshape(PLACES // 2, 128), to_box[...])
        if t == 0:
            for q in range(4):
                faces[1, q // 2, q % 2] = grid[0:56, 128 * q : 128 * q + 128]
            for copy in halos[1]:
                copy.start()
        else:
            for q in range(4):
                grid_out[pl.ds(q, NS, stride=4), :] = grid[0:NS, 128 * q : 128 * q + 128]
    for copy in stores:
        copy.wait()
    for t in range(2):
        for copy in halos[t]:
            copy.wait_send()
        await_row(f_send, t, fs_sem)
        await_row(s_send, t, ss_sem)
    await_all(moving.at[pl.ds(0, DEVICES - 1)], move_send.at[0])
    await_all(r_moving.at[pl.ds(0, DEVICES - 1)], move_send.at[1])


def per_device(
    grid_scalars, axial_speed, particles, cell_owner, cell_slot, mix_rate, partner,
    chem_input, chem_hidden, chem_output, react_slots, react_count, leave_slots, arrive_slots,
):
    vmem = pl.BlockSpec(memory_space=pltpu.VMEM)
    hbm = pl.BlockSpec(memory_space=pl.ANY)
    dma = pltpu.SemaphoreType.DMA
    messages = pltpu.VMEM((2, OWNERS, HALF, 128), F32)
    cells = pltpu.VMEM((DEVICES, 2, 14, 128), F32)
    short = pltpu.VMEM((DEVICES, 1, 128), F32)
    grid, out = pl.pallas_call(
        step_kernel,
        out_shape=(
            jax.ShapeDtypeStruct((4 * NS, 128), F32),
            jax.ShapeDtypeStruct((ROWS, CELLS), F32),
        ),
        in_specs=[vmem, vmem, hbm] + [vmem] * 11,
        out_specs=(vmem, hbm),
        scratch_shapes=[
            pltpu.VMEM((4, ROWS, 128), F32),
            pltpu.VMEM((2, ROWS, 128), F32),
            pltpu.VMEM((2, 2, 2, 56, 128), F32),
            pltpu.VMEM((2, 4, 2, 56, 128), F32),
            messages,
            messages,
            messages,
            messages,
            cells,
            cells,
            short,
            short,
            pltpu.VMEM((PLACES, CELLS), BF16),
            pltpu.VMEM((PLACES, CELLS), BF16),
            pltpu.VMEM((CELLS, CELLS), BF16),
            pltpu.VMEM((CELLS + LIST, CELLS), BF16),
            pltpu.VMEM((4, LIST, 128), F32),
            pltpu.VMEM((2, NP, CELLS), jnp.int32),
            pltpu.VMEM((CHAINS * WIDE, 64, LIST), F32),
            pltpu.VMEM((64, CELLS), F32),
            pltpu.VMEM((2, 64, 128), F32),
            pltpu.VMEM((64, LIST), F32),
            pltpu.VMEM((ROWS, CELLS), F32),
            pltpu.VMEM((128, 256), F32),
            pltpu.VMEM((64, 256), F32),
            dma((4,)),
            dma((ROWS // SPAN,)),
            dma((2, 4)),
            dma((2, 4)),
            dma((2,)),
            dma((2,)),
            dma((2,)),
            dma((2,)),
            dma((2,)),
            dma((2,)),
        ],
        compiler_params=pltpu.CompilerParams(
            collective_id=0, has_side_effects=True, vmem_limit_bytes=VMEM_LIMIT
        ),
        name="step",
    )(
        grid_scalars.reshape(4 * NS, 128),
        axial_speed.reshape(4, 128),
        particles.reshape(ROWS, CELLS),
        cell_owner.reshape(4, 128),
        cell_slot.reshape(4, 128),
        mix_rate.reshape(1, CELLS),
        partner,
        chem_input.T,
        chem_hidden,
        chem_output,
        react_slots,
        react_count.reshape(1, 1),
        leave_slots,
        arrive_slots,
    )
    return grid.reshape(grid_scalars.shape), out.reshape(particles.shape)


def solution(mesh):
    placed = (
        P(None, "gx", "gy", None),
        P("gx", "gy", None),
        P(None, None, ("gx", "gy")),
        P("gx", "gy", None),
        P("gx", "gy", None),
        P(("gx", "gy")),
        P(None, ("gx", "gy")),
        P(),
        P(),
        P(),
        P(("gx", "gy"), None),
        P(("gx", "gy")),
        P(("gx", "gy"), None),
        P(("gx", "gy"), None),
    )
    return jax.shard_map(
        per_device,
        mesh=mesh,
        in_specs=placed,
        out_specs=(P(None, "gx", "gy", None), P(None, None, ("gx", "gy"))),
        check_vma=False,
    )
```

time: 128 us -> 112 us (0.88)
  the two profiles are of different devices: /device:TPU:1 before, /device:TPU:5 now
where the time goes in v2:
time: 112 us
  Pallas kernels  105 us (94%)
  local copies, waits for them, and re-layouts  5.99 us (5%)
  between operations  1.29 us (1%)
    pallas_call x1, Pallas kernels, per_device(): pl.pallas_call(step_kernel, out_shape=(jax.ShapeDtypeStruct((4 * NS, 128)...  105 us
    unnamed x2, local copies, waits for them, and re-layouts  5.99 us

profile of v2, /device:TPU:5, one launch (start us, length us, event | category | flops | bytes accessed | tf_op | source)
XLA Modules:
  0.0 112.0 jit_solution(17952488825768651181)
XLA Ops:
  1.3 104.7 %step.1 = (f32[216,128]{1,0:T(8,128)}, f32[1728,512]{1,0:T(8,128)}) custom-call(f32[216,128]{1,0:T(8,128)} %bitcast.13, f32[4,128]{1,0:T(4,128)} %bitcast.16, f32[1728,512]{1,0:T(8,128)} %bitcast.11, s32[4,128]{1,0:T(4,128)} %bitcast.17, s32[4,128]{1,0:T(4,128)} %bitcast.18, f32[1,512]{1,0:T(1,128)} %bitcast.19, s32[32,512]{1,0:T(8,128)} %partner.1, ...), custom_call_target="tpu_custom_call" | custom-call | tf_op jit(solution)/shard_map/step/pallas_call | solution.py:405
  106.0 1.5 %copy.19 = f32[54,2,2,128]{3,2,1,0:T(2,128)} copy(f32[54,2,2,128]{3,2,1,0:T(2,128)} %bitcast.14) | data formatting | bytes 221184
  107.6 4.4 %copy.20 = f32[54,32,512]{2,1,0:T(8,128)} copy(f32[54,32,512]{2,1,0:T(8,128)} %bitcast.12) | data formatting | bytes 7077888

commit v3 on v2

--- a/solution.py
+++ b/solution.py
@@ -17,6 +17,8 @@
 PLACES = 2 * OWNERS * HALF
 LIST = 256
 SPAN = 432
+STRIDE = 37
+PACE = (7, 33, 60)
 CHAINS, WIDE = 2, 4
 LABEL = 54
 VMEM_LIMIT = 56 * 1024 * 1024
@@ -37,8 +39,8 @@
 
 
 def silu(a):
-    h = 0.5 * a
-    return (h + h * jnp.tanh(h)).astype(BF16)
+    h = (0.5 * a).astype(BF16)
+    return h + h * jnp.tanh(h)
 
 
 def packed(picker, values):
@@ -125,9 +127,9 @@
         lax.fori_loop(1, OWNERS, send, 0)
         into[t, gy] = out[t, gy]
 
-    def exchange_all(out, into, i):
+    def exchange_all(out, into, i, first=1, last=DEVICES):
         def send(k, carry):
-            other, where = device(k)
+            other, where = device(lax.rem(k * STRIDE, DEVICES))
             pltpu.make_async_remote_copy(
                 src_ref=out.at[other],
                 dst_ref=into.at[me],
@@ -138,8 +140,9 @@
             ).start()
             return carry
 
-        lax.fori_loop(1, DEVICES, send, 0)
-        into[me] = out[me]
+        lax.fori_loop(first, last, send, 0)
+        if first == 1:
+            into[me] = out[me]
 
     def await_all(part, sem):
         pltpu.make_async_copy(part, part, sem).wait()
@@ -275,6 +278,8 @@
         for j in range(OWNERS):
             f_send[t, j] = message[HALF * j : HALF * j + HALF]
         exchange(f_send, f_recv, t, fs_sem, fr_sem)
+        if t == 1:
+            exchange_all(moving, moved, 0, PACE[1], PACE[2])
         if t == 0:
             for copy in loads:
                 copy.wait()
@@ -318,6 +323,7 @@
             both = both + pltpu.roll(both, 64, axis=1)
             r_moving[:, 0, :] = jnp.where(iota((DEVICES, 128), 1) < 64, both[:DEVICES], both[DEVICES:])
             exchange_all(r_moving, r_moved, 1)
+            exchange_all(moving, moved, 0, PACE[2], DEVICES)
         total = chemistry(state, keep_row[:, 0:LIST], r_f, live_row)
         source = through(total * (1.0 / NP), order[:, 0:LIST], mat_nt)
         message = packed(to_slot[...], source)
@@ -335,7 +341,7 @@
             hi, lo = split(jnp.concatenate([rows_of(state, 4, 1664, 64), extra], axis=0))
             value = mat_nt(goes, hi) + mat_nt(goes, lo)
             moving[:, :, 13, :] = value.reshape(DEVICES, 2, 128)
-            exchange_all(moving, moved, 0)
+            exchange_all(moving, moved, 0, 1, PACE[0])
         else:
             await_all(moved.at[pl.ds(0, DEVICES - 1)], move_recv.at[0])
             await_all(r_moved.at[pl.ds(0, DEVICES - 1)], move_recv.at[1])
@@ -378,6 +384,7 @@
                 faces[1, q // 2, q % 2] = grid[0:56, 128 * q : 128 * q + 128]
             for copy in halos[1]:
                 copy.start()
+            exchange_all(moving, moved, 0, PACE[0], PACE[1])
         else:
             for q in range(4):
                 grid_out[pl.ds(q, NS, stride=4), :] = grid[0:NS, 128 * q : 128 * q + 128]

time: 112 us -> 90 us (0.80)
  the two profiles are of different devices: /device:TPU:5 before, /device:TPU:1 now
where the time goes in v3:
time: 90 us; the launch traced here: 89.8 us
  Pallas kernels  82.5 us (92%)
  local copies, waits for them, and re-layouts  5.99 us (7%)
  between operations  1.29 us (1%)
    pallas_call x1, Pallas kernels, per_device(): pl.pallas_call(step_kernel, out_shape=(jax.ShapeDtypeStruct((4 * NS, 128)...  82.5 us
    unnamed x2, local copies, waits for them, and re-layouts  5.99 us

profile of v3, /device:TPU:1, one launch (start us, length us, event | category | flops | bytes accessed | tf_op | source)
XLA Modules:
  0.0 89.8 jit_solution(7701742509997024411)
XLA Ops:
  1.3 82.5 %step.1 = (f32[216,128]{1,0:T(8,128)}, f32[1728,512]{1,0:T(8,128)}) custom-call(f32[216,128]{1,0:T(8,128)} %bitcast.13, f32[4,128]{1,0:T(4,128)} %bitcast.16, f32[1728,512]{1,0:T(8,128)} %bitcast.11, s32[4,128]{1,0:T(4,128)} %bitcast.17, s32[4,128]{1,0:T(4,128)} %bitcast.18, f32[1,512]{1,0:T(1,128)} %bitcast.19, s32[32,512]{1,0:T(8,128)} %partner.1, ...), custom_call_target="tpu_custom_call" | custom-call | tf_op jit(solution)/shard_map/step/pallas_call | solution.py:412
  83.8 1.5 %copy.19 = f32[54,2,2,128]{3,2,1,0:T(2,128)} copy(f32[54,2,2,128]{3,2,1,0:T(2,128)} %bitcast.14) | data formatting | bytes 221184
  85.3 4.4 %copy.20 = f32[54,32,512]{2,1,0:T(8,128)} copy(f32[54,32,512]{2,1,0:T(8,128)} %bitcast.12) | data formatting | bytes 7077888

commit v4 on v3

--- a/solution.py
+++ b/solution.py
@@ -18,7 +18,7 @@
 LIST = 256
 SPAN = 432
 STRIDE = 37
-PACE = (7, 33, 60)
+PACE = (30, 60)
 CHAINS, WIDE = 2, 4
 LABEL = 54
 VMEM_LIMIT = 56 * 1024 * 1024
@@ -39,8 +39,7 @@
 
 
 def silu(a):
-    h = (0.5 * a).astype(BF16)
-    return h + h * jnp.tanh(h)
+    return (a + a * jnp.tanh(a)).astype(BF16)
 
 
 def packed(picker, values):
@@ -63,7 +62,7 @@
     grid_in, speed, parts_in, owner, slot, rate, partner, w_in, w_hid, w_out, listed, count, leave, arrive,
     grid_out, parts_out,
     state, guest, faces, halo, f_send, f_recv, s_send, s_recv, moving, moved, r_moving, r_moved,
-    to_box, to_slot, order, final, turn, mates, feed, r_f, r_late, r_g, made, wi, wo,
+    to_box, to_slot, order, final, turn, goes_halves, mates, feed, r_f, r_late, r_g, made, wi, wo,
     load_sem, store_sem, halo_send, halo_recv, fs_sem, fr_sem, ss_sem, sr_sem, move_send, move_recv,
 ):
     gx, gy = lax.axis_index("gx"), lax.axis_index("gy")
@@ -127,12 +126,12 @@
         lax.fori_loop(1, OWNERS, send, 0)
         into[t, gy] = out[t, gy]
 
-    def exchange_all(out, into, i, first=1, last=DEVICES):
+    def exchange_all(out, into, c, i, first=1, last=DEVICES):
         def send(k, carry):
             other, where = device(lax.rem(k * STRIDE, DEVICES))
             pltpu.make_async_remote_copy(
-                src_ref=out.at[other],
-                dst_ref=into.at[me],
+                src_ref=out.at[c, other],
+                dst_ref=into.at[c, me],
                 send_sem=move_send.at[i],
                 recv_sem=move_recv.at[i],
                 device_id=where,
@@ -142,7 +141,10 @@
 
         lax.fori_loop(first, last, send, 0)
         if first == 1:
-            into[me] = out[me]
+            into[c, me] = out[c, me]
+
+    def await_cells(buf, c, sem):
+        await_all(buf.at[c, pl.ds(0, DEVICES - 1)], sem)
 
     def await_all(part, sem):
         pltpu.make_async_copy(part, part, sem).wait()
@@ -180,32 +182,45 @@
     wo[...] = jnp.zeros_like(wo)
     wo[0:NS, :] = w_out[...].astype(F32)
     feed[...] = jnp.zeros_like(feed)
-    weights_in = wi[...].T[:, 0:64].astype(BF16)
+    weights_in = (0.5 * wi[...].T[:, 0:64]).astype(BF16)
+    weights_hid = (0.5 * w_hid[...].astype(F32)).astype(BF16)
     weights_out = wo[...].astype(BF16)
-    mates[0] = partner[...]
-
-    def mix(t, keep_row):
-        for lb in range(4):
-            cols = slice(128 * lb, 128 * lb + 128)
-            index = [mates[t, 8 * o : 8 * o + 8, cols] & 7 for o in range(4)]
-            group = [mates[t, 8 * o : 8 * o + 8, cols] >> 3 for o in range(4)]
-            late = t == 1 and lb >= 2
-
-            def body(s, carry):
-                base = pl.multiple_of(s * NP, NP)
-                tiles = [state[lb, pl.ds(base + 8 * g, 8), :] for g in range(4)]
-                for o in range(4):
-                    mate = jnp.take_along_axis(tiles[0], index[o], axis=0, mode="promise_in_bounds")
-                    for g in range(1, 4):
-                        other = jnp.take_along_axis(tiles[g], index[o], axis=0, mode="promise_in_bounds")
-                        mate = jnp.where(group[o] == g, other, mate)
-                    mixed = 0.6 * tiles[o] + 0.4 * mate
-                    if late:
-                        mixed = mixed * keep_row[:, cols] + r_late[lb - 2, pl.ds(s, 1), :]
-                    state[lb, pl.ds(base + 8 * o, 8), :] = mixed
-                return carry
-
-            lax.fori_loop(0, NS, body, 0, unroll=2)
+
+    def mix(ref, lb, mate_of, keep=None, late=None):
+        index = [mate_of[8 * o : 8 * o + 8] & 7 for o in range(4)]
+        group = [mate_of[8 * o : 8 * o + 8] >> 3 for o in range(4)]
+
+        def body(s, carry):
+            base = pl.multiple_of(s * NP, NP)
+            tiles = [ref[lb, pl.ds(base + 8 * g, 8), :] for g in range(4)]
+            for o in range(4):
+                mate = jnp.take_along_axis(tiles[0], index[o], axis=0, mode="promise_in_bounds")
+                for g in range(1, 4):
+                    other = jnp.take_along_axis(tiles[g], index[o], axis=0, mode="promise_in_bounds")
+                    mate = jnp.where(group[o] == g, other, mate)
+                mixed = 0.6 * tiles[o] + 0.4 * mate
+                if keep is not None:
+                    mixed = mixed * keep + r_late[late, pl.ds(s, 1), :]
+                ref[lb, pl.ds(base + 8 * o, 8), :] = mixed
+            return carry
+
+        lax.fori_loop(0, NS, body, 0, unroll=2)
+
+    def pack_cells(c, goes_c, extra):
+        for j in range(14):
+            if j < 13:
+                value = rows_of(state, 4, 128 * j, 128)
+            else:
+                value = jnp.concatenate([rows_of(state, 4, 1664, 64), extra], axis=0)
+            hi, lo = split(value)
+            moving[c, :, j, :] = mat_nt(goes_c, hi) + mat_nt(goes_c, lo)
+
+    def unpack_cells(c):
+        for j in range(14):
+            block = moved[c, :, j, :].T
+            size = min(128, ROWS - 128 * j)
+            guest[c, 128 * j : 128 * j + size, :] = block[0:size]
+        return block[64:72], block[96:128]
 
     def rows_of(ref, blocks, start, size):
         return jnp.concatenate([ref[lb, start : start + size, :] for lb in range(blocks)], axis=1)
@@ -236,41 +251,61 @@
                 done.append(center + 0.1 * (around - 6.0 * center) - speed[q : q + 1, :] * (center - up))
         return jnp.concatenate(done, axis=1)
 
-    def chemistry(ref, keep, source, live):
+    def chemistry(ref, blocks, keep, source, live):
+        width = 128 * blocks
+        wide = WIDE * 2 // blocks
+        chains = range(CHAINS)
+
         def body(g, total):
-            for c in range(CHAINS):
-                for i in range(WIDE):
-                    p = (CHAINS * g + c) * WIDE + i
-                    own = jnp.concatenate([ref[lb, pl.ds(p, NS, stride=NP), :] for lb in range(2)], axis=1)
-                    feed[c * WIDE + i, 0:NS, :] = own * keep + source[0:NS, 0:LIST]
+            for c in chains:
+                for i in range(wide):
+                    p = (CHAINS * g + c) * wide + i
+                    own = jnp.concatenate([ref[lb, pl.ds(p, NS, stride=NP), :] for lb in range(blocks)], axis=1)
+                    feed[c * wide + i, 0:NS, 0:width] = own * keep + source[0:NS, 0:width]
             columns = [
                 jnp.concatenate(
-                    [jnp.where(live > 0.5, feed[c * WIDE + i], 0.0).astype(BF16) for i in range(WIDE)], axis=1
+                    [
+                        jnp.where(live > 0.5, feed[c * wide + i, :, 0:width], 0.0).astype(BF16)
+                        for i in range(wide)
+                    ],
+                    axis=1,
                 )
-                for c in range(CHAINS)
+                for c in chains
             ]
             one = [silu(mat(weights_in, x)) for x in columns]
-            two = [silu(mat(w_hid[...], x)) for x in one]
+            two = [silu(mat(weights_hid, x)) for x in one]
             change = [mat(weights_out, x).astype(BF16).astype(F32) for x in two]
-            for c in range(CHAINS):
-                for i in range(WIDE):
-                    p = (CHAINS * g + c) * WIDE + i
-                    part = jnp.where(live > 0.5, change[c][:, LIST * i : LIST * i + LIST], 0.0)
-                    done = feed[c * WIDE + i] + part
-                    for lb in range(2):
+            for c in chains:
+                for i in range(wide):
+                    p = (CHAINS * g + c) * wide + i
+                    part = jnp.where(live > 0.5, change[c][:, width * i : width * i + width], 0.0)
+                    done = feed[c * wide + i, :, 0:width] + part
+                    for lb in range(blocks):
                         ref[lb, pl.ds(p, NS, stride=NP), :] = done[0:NS, 128 * lb : 128 * lb + 128]
                     total = total + part
             return total
 
-        return lax.fori_loop(0, NP // (CHAINS * WIDE), body, jnp.zeros((64, LIST), F32))
+        return lax.fori_loop(0, NP // (CHAINS * wide), body, jnp.zeros((64, width), F32))
 
     def through(values, matrix, product=mat):
         hi, lo = split(values)
         both = product(jnp.concatenate([hi, lo], axis=0), matrix)
         return both[: values.shape[0]] + both[values.shape[0] :]
 
+    for copy in loads[0:2]:
+        copy.wait()
+    for lb in range(2):
+        mix(state, lb, partner[:, 128 * lb : 128 * lb + 128])
     row = iota((64, CELLS), 0)
     for t in range(2):
+        if t == 1:
+            await_cells(moved, 0, move_recv.at[0])
+            await_cells(r_moved, 0, move_recv.at[2])
+            meta, mate_of = unpack_cells(0)
+            r_g[:, 0:128] = r_moved[0].reshape(DEVICES, 128).T[0:64]
+            guest_keep, guest_live = 1.0 - meta[0:1], meta[1:2]
+            guest_mates = mate_of.astype(jnp.int32)
+            chemistry(guest, 1, guest_keep, r_g, guest_live)
         for copy in halos[t]:
             copy.wait_recv()
         grid = jnp.concatenate([transport(t), jnp.zeros((8, CELLS), F32)], axis=0)
@@ -278,31 +313,38 @@
         for j in range(OWNERS):
             f_send[t, j] = message[HALF * j : HALF * j + HALF]
         exchange(f_send, f_recv, t, fs_sem, fr_sem)
-        if t == 1:
-            exchange_all(moving, moved, 0, PACE[1], PACE[2])
         if t == 0:
-            for copy in loads:
+            for copy in loads[2:4]:
                 copy.wait()
-            mix(0, None)
+            for lb in range(2, 4):
+                mix(state, lb, partner[:, 128 * lb : 128 * lb + 128])
             permute()
-            mates[1] = mat(partner[...].astype(F32).astype(BF16), order[...]).astype(jnp.int32)
+            mates_now = mat(partner[...].astype(F32).astype(BF16), order[...])
             rate_row = through(jnp.broadcast_to(rate[...], (8, CELLS)), order[...])[0:1]
             keep_row = 1.0 - rate_row
             goes = (iota((CELLS, LIST), 0) == leave[...]).astype(F32)
             goes = mat(goes.T.astype(BF16), order[...])
             for lb in range(4):
                 turn[lb] = goes[:, 128 * lb : 128 * lb + 128]
-            halves = [
-                jnp.concatenate([turn[lb, pl.ds(c, DEVICES, stride=2), :] for lb in range(4)], axis=1) for c in range(2)
-            ]
-            goes_halves = jnp.concatenate(halves, axis=0).astype(BF16)
-            goes = goes.astype(BF16)
+            for c in range(2):
+                goes_halves[DEVICES * c : DEVICES * c + DEVICES, :] = jnp.concatenate(
+                    [turn[lb, pl.ds(c, DEVICES, stride=2), :] for lb in range(4)], axis=1
+                ).astype(BF16)
+            live_all = jnp.concatenate([live_row, jnp.zeros((1, LIST), F32)], axis=1)
+            extra = jnp.where(row == 0, rate_row, jnp.where(row == 1, live_all, 0.0))
+            extra = jnp.concatenate([extra[0:32], mates_now], axis=0)
+            mates[...] = extra
+            pack_cells(0, goes_halves[0:DEVICES], extra)
+            exchange_all(moving, moved, 0, 0)
+        else:
+            exchange_all(moving, moved, 1, 1, PACE[0], PACE[1])
+            mix(guest, 0, guest_mates)
             lands = (iota((CELLS, LIST), 0) == arrive[...]).astype(F32)
             taken = mat_nt(jnp.ones((8, LIST), BF16), lands.astype(BF16))[0:1]
             lands = lands.T
             for lb in range(4):
                 turn[lb] = lands[:, 128 * lb : 128 * lb + 128]
-            final[0:CELLS, :] = jnp.where(taken > 0.5, 0.0, chosen.T).astype(BF16)
+            final[0:CELLS, :] = jnp.where(taken > 0.5, 0.0, order[...].astype(F32).T).astype(BF16)
             for c in range(2):
                 final[CELLS + DEVICES * c : CELLS + DEVICES * (c + 1), :] = jnp.concatenate(
                     [turn[lb, pl.ds(c, DEVICES, stride=2), :] for lb in range(4)], axis=1
@@ -317,45 +359,37 @@
         r_f[...] = through(unpacked(arrived, to_slot[...]), order[...]) * rate_row
         for lb in range(2):
             r_late[lb] = r_f[:, LIST + 128 * lb : LIST + 128 * lb + 128]
+        hi, lo = split(r_f[...])
+        both = mat_nt(goes_halves[...], jnp.concatenate([hi, lo], axis=0))
+        both = both + pltpu.roll(both, 64, axis=1)
+        r_moving[t, :, 0, :] = jnp.where(iota((DEVICES, 128), 1) < 64, both[:DEVICES], both[DEVICES:])
+        exchange_all(r_moving, r_moved, t, 2 + t)
         if t == 1:
-            hi, lo = split(r_f[...])
-            both = mat_nt(goes_halves, jnp.concatenate([hi, lo], axis=0))
-            both = both + pltpu.roll(both, 64, axis=1)
-            r_moving[:, 0, :] = jnp.where(iota((DEVICES, 128), 1) < 64, both[:DEVICES], both[DEVICES:])
-            exchange_all(r_moving, r_moved, 1)
-            exchange_all(moving, moved, 0, PACE[2], DEVICES)
-        total = chemistry(state, keep_row[:, 0:LIST], r_f, live_row)
+            exchange_all(moving, moved, 1, 1, PACE[1], DEVICES)
+        total = chemistry(state, 2, keep_row[:, 0:LIST], r_f, live_row)
         source = through(total * (1.0 / NP), order[:, 0:LIST], mat_nt)
         message = packed(to_slot[...], source)
         for j in range(OWNERS):
             s_send[t, j] = message[HALF * j : HALF * j + HALF]
         exchange(s_send, s_recv, t, ss_sem, sr_sem)
         if t == 0:
-            mix(1, keep_row)
-            for j in range(13):
-                hi, lo = split(rows_of(state, 4, 128 * j, 128))
-                value = mat_nt(goes, hi) + mat_nt(goes, lo)
-                moving[:, :, j, :] = value.reshape(DEVICES, 2, 128)
-            live_all = jnp.concatenate([live_row, jnp.zeros((1, LIST), F32)], axis=1)
-            extra = jnp.where(row == 0, rate_row, jnp.where(row == 1, live_all, 0.0))
-            hi, lo = split(jnp.concatenate([rows_of(state, 4, 1664, 64), extra], axis=0))
-            value = mat_nt(goes, hi) + mat_nt(goes, lo)
-            moving[:, :, 13, :] = value.reshape(DEVICES, 2, 128)
-            exchange_all(moving, moved, 0, 1, PACE[0])
+            for lb in range(4):
+                cols = slice(128 * lb, 128 * lb + 128)
+                mate_of = mates[32:64, cols].astype(jnp.int32)
+                if lb < 2:
+                    mix(state, lb, mate_of)
+                else:
+                    mix(state, lb, mate_of, keep_row[:, cols], lb - 2)
+            pack_cells(1, goes_halves[DEVICES:], mates[...])
         else:
-            await_all(moved.at[pl.ds(0, DEVICES - 1)], move_recv.at[0])
-            await_all(r_moved.at[pl.ds(0, DEVICES - 1)], move_recv.at[1])
-            metas = []
-            for c in range(2):
-                for j in range(14):
-                    block = moved[:, c, j, :].T
-                    size = min(128, ROWS - 128 * j)
-                    guest[c, 128 * j : 128 * j + size, :] = block[0:size]
-                metas.append(block[64:72])
-            metas = jnp.concatenate(metas, axis=1)
-            r_turned = r_moved[...].reshape(DEVICES, 128).T
+            await_cells(moved, 1, move_recv.at[1])
+            await_cells(r_moved, 1, move_recv.at[3])
+            late_meta, _ = unpack_cells(1)
+            r_turned = r_moved[1].reshape(DEVICES, 128).T
             r_g[...] = jnp.concatenate([r_turned[0:64], r_turned[64:128]], axis=1)
-            chemistry(guest, 1.0 - metas[0:1], r_g, metas[1:2])
+            guest_keep = jnp.concatenate([guest_keep, 1.0 - late_meta[0:1]], axis=1)
+            guest_live = jnp.concatenate([guest_live, late_meta[1:2]], axis=1)
+            chemistry(guest, 2, guest_keep, r_g, guest_live)
 
             def relax(s, carry):
                 base = pl.multiple_of(s * NP, NP)
@@ -384,7 +418,7 @@
                 faces[1, q // 2, q % 2] = grid[0:56, 128 * q : 128 * q + 128]
             for copy in halos[1]:
                 copy.start()
-            exchange_all(moving, moved, 0, PACE[0], PACE[1])
+            exchange_all(moving, moved, 1, 1, 1, PACE[0])
         else:
             for q in range(4):
                 grid_out[pl.ds(q, NS, stride=4), :] = grid[0:NS, 128 * q : 128 * q + 128]
@@ -395,8 +429,8 @@
             copy.wait_send()
         await_row(f_send, t, fs_sem)
         await_row(s_send, t, ss_sem)
-    await_all(moving.at[pl.ds(0, DEVICES - 1)], move_send.at[0])
-    await_all(r_moving.at[pl.ds(0, DEVICES - 1)], move_send.at[1])
+        await_cells(moving, t, move_send.at[t])
+        await_cells(r_moving, t, move_send.at[2 + t])
 
 
 def per_device(
@@ -407,8 +441,8 @@
     hbm = pl.BlockSpec(memory_space=pl.ANY)
     dma = pltpu.SemaphoreType.DMA
     messages = pltpu.VMEM((2, OWNERS, HALF, 128), F32)
-    cells = pltpu.VMEM((DEVICES, 2, 14, 128), F32)
-    short = pltpu.VMEM((DEVICES, 1, 128), F32)
+    cells = pltpu.VMEM((2, DEVICES, 14, 128), F32)
+    short = pltpu.VMEM((2, DEVICES, 1, 128), F32)
     grid, out = pl.pallas_call(
         step_kernel,
         out_shape=(
@@ -435,8 +469,9 @@
             pltpu.VMEM((CELLS, CELLS), BF16),
             pltpu.VMEM((CELLS + LIST, CELLS), BF16),
             pltpu.VMEM((4, LIST, 128), F32),
-            pltpu.VMEM((2, NP, CELLS), jnp.int32),
-            pltpu.VMEM((CHAINS * WIDE, 64, LIST), F32),
+            pltpu.VMEM((LIST, CELLS), BF16),
+            pltpu.VMEM((64, CELLS), F32),
+            pltpu.VMEM((CHAINS * WIDE * 2, 64, LIST), F32),
             pltpu.VMEM((64, CELLS), F32),
             pltpu.VMEM((2, 64, 128), F32),
             pltpu.VMEM((64, LIST), F32),
@@ -451,8 +486,8 @@
             dma((2,)),
             dma((2,)),
             dma((2,)),
-            dma((2,)),
-            dma((2,)),
+            dma((4,)),
+            dma((4,)),
         ],
         compiler_params=pltpu.CompilerParams(
             collective_id=0, has_side_effects=True, vmem_limit_bytes=VMEM_LIMIT

time: 90 us -> 86.6 us (0.962)
  Pallas kernels: 82.5 us -> 79.2 us
    pallas_call x1, Pallas kernels: 82.5 us -> 79.2 us  [per_device(): pl.pallas_call(step_kernel, out_shape=(jax.ShapeDtypeStruct((4 * NS, 128)...]
where the time goes in v4:
time: 86.6 us; the launch traced here: 86.4 us
  Pallas kernels  79.2 us (91%)
  local copies, waits for them, and re-layouts  5.99 us (7%)
  between operations  1.29 us (1%)
    pallas_call x1, Pallas kernels, per_device(): pl.pallas_call(step_kernel, out_shape=(jax.ShapeDtypeStruct((4 * NS, 128)...  79.2 us
    unnamed x2, local copies, waits for them, and re-layouts  5.99 us

profile of v4, /device:TPU:1, one launch (start us, length us, event | category | flops | bytes accessed | tf_op | source)
XLA Modules:
  0.0 86.4 jit_solution(11734818024505648924)
XLA Ops:
  1.3 79.2 %step.1 = (f32[216,128]{1,0:T(8,128)}, f32[1728,512]{1,0:T(8,128)}) custom-call(f32[216,128]{1,0:T(8,128)} %bitcast.13, f32[4,128]{1,0:T(4,128)} %bitcast.16, f32[1728,512]{1,0:T(8,128)} %bitcast.11, s32[4,128]{1,0:T(4,128)} %bitcast.17, s32[4,128]{1,0:T(4,128)} %bitcast.18, f32[1,512]{1,0:T(1,128)} %bitcast.19, s32[32,512]{1,0:T(8,128)} %partner.1, ...), custom_call_target="tpu_custom_call" | custom-call | tf_op jit(solution)/shard_map/step/pallas_call | solution.py:446
  80.5 1.5 %copy.19 = f32[54,2,2,128]{3,2,1,0:T(2,128)} copy(f32[54,2,2,128]{3,2,1,0:T(2,128)} %bitcast.14) | data formatting | bytes 221184
  82.0 4.4 %copy.20 = f32[54,32,512]{2,1,0:T(8,128)} copy(f32[54,32,512]{2,1,0:T(8,128)} %bitcast.12) | data formatting | bytes 7077888

commit v5 on v4

--- a/solution.py
+++ b/solution.py
@@ -18,6 +18,7 @@
 LIST = 256
 SPAN = 432
 STRIDE = 37
+EARLY = 90
 PACE = (30, 60)
 CHAINS, WIDE = 2, 4
 LABEL = 54
@@ -305,7 +306,16 @@
             r_g[:, 0:128] = r_moved[0].reshape(DEVICES, 128).T[0:64]
             guest_keep, guest_live = 1.0 - meta[0:1], meta[1:2]
             guest_mates = mate_of.astype(jnp.int32)
-            chemistry(guest, 1, guest_keep, r_g, guest_live)
+            lands = (iota((CELLS, LIST), 0) == arrive[...]).astype(F32)
+            taken = mat_nt(jnp.ones((8, LIST), BF16), lands.astype(BF16))[0:1]
+            lands = lands.T
+            for lb in range(4):
+                turn[lb] = lands[:, 128 * lb : 128 * lb + 128]
+            final[0:CELLS, :] = jnp.where(taken > 0.5, 0.0, order[...].astype(F32).T).astype(BF16)
+            for c in range(2):
+                final[CELLS + DEVICES * c : CELLS + DEVICES * (c + 1), :] = jnp.concatenate(
+                    [turn[lb, pl.ds(c, DEVICES, stride=2), :] for lb in range(4)], axis=1
+                ).astype(BF16)
         for copy in halos[t]:
             copy.wait_recv()
         grid = jnp.concatenate([transport(t), jnp.zeros((8, CELLS), F32)], axis=0)
@@ -335,20 +345,11 @@
             extra = jnp.concatenate([extra[0:32], mates_now], axis=0)
             mates[...] = extra
             pack_cells(0, goes_halves[0:DEVICES], extra)
-            exchange_all(moving, moved, 0, 0)
+            exchange_all(moving, moved, 0, 0, 1, EARLY)
         else:
             exchange_all(moving, moved, 1, 1, PACE[0], PACE[1])
+            chemistry(guest, 1, guest_keep, r_g, guest_live)
             mix(guest, 0, guest_mates)
-            lands = (iota((CELLS, LIST), 0) == arrive[...]).astype(F32)
-            taken = mat_nt(jnp.ones((8, LIST), BF16), lands.astype(BF16))[0:1]
-            lands = lands.T
-            for lb in range(4):
-                turn[lb] = lands[:, 128 * lb : 128 * lb + 128]
-            final[0:CELLS, :] = jnp.where(taken > 0.5, 0.0, order[...].astype(F32).T).astype(BF16)
-            for c in range(2):
-                final[CELLS + DEVICES * c : CELLS + DEVICES * (c + 1), :] = jnp.concatenate(
-                    [turn[lb, pl.ds(c, DEVICES, stride=2), :] for lb in range(4)], axis=1
-                ).astype(BF16)
         await_row(f_recv, t, fr_sem)
         arrived = f_recv[t].reshape(PLACES // 2, 128)
         if t == 0:
@@ -363,8 +364,8 @@
         both = mat_nt(goes_halves[...], jnp.concatenate([hi, lo], axis=0))
         both = both + pltpu.roll(both, 64, axis=1)
         r_moving[t, :, 0, :] = jnp.where(iota((DEVICES, 128), 1) < 64, both[:DEVICES], both[DEVICES:])
-        exchange_all(r_moving, r_moved, t, 2 + t)
         if t == 1:
+            exchange_all(r_moving, r_moved, 1, 3)
             exchange_all(moving, moved, 1, 1, PACE[1], DEVICES)
         total = chemistry(state, 2, keep_row[:, 0:LIST], r_f, live_row)
         source = through(total * (1.0 / NP), order[:, 0:LIST], mat_nt)
@@ -373,6 +374,8 @@
             s_send[t, j] = message[HALF * j : HALF * j + HALF]
         exchange(s_send, s_recv, t, ss_sem, sr_sem)
         if t == 0:
+            exchange_all(moving, moved, 0, 0, EARLY, DEVICES)
+            exchange_all(r_moving, r_moved, 0, 2)
             for lb in range(4):
                 cols = slice(128 * lb, 128 * lb + 128)
                 mate_of = mates[32:64, cols].astype(jnp.int32)
@@ -382,6 +385,19 @@
                     mix(state, lb, mate_of, keep_row[:, cols], lb - 2)
             pack_cells(1, goes_halves[DEVICES:], mates[...])
         else:
+            def relax(s, carry):
+                base = pl.multiple_of(s * NP, NP)
+                for lb in range(2, 4):
+                    cols = slice(128 * lb, 128 * lb + 128)
+                    span = pl.ds(base, NP)
+                    state[lb, span, :] = state[lb, span, :] * keep_row[:, cols] + r_late[lb - 2, pl.ds(s, 1), :]
+                return carry
+
+            lax.fori_loop(0, NS, relax, 0)
+            for k in range(ROWS // SPAN):
+                hi, lo = split(rows_of(state, 4, SPAN * k, SPAN))
+                own = final[0:CELLS, :]
+                made[SPAN * k : SPAN * k + SPAN, :] = mat(hi, own) + mat(lo, own)
             await_cells(moved, 1, move_recv.at[1])
             await_cells(r_moved, 1, move_recv.at[3])
             late_meta, _ = unpack_cells(1)
@@ -391,15 +407,6 @@
             guest_live = jnp.concatenate([guest_live, late_meta[1:2]], axis=1)
             chemistry(guest, 2, guest_keep, r_g, guest_live)
 
-            def relax(s, carry):
-                base = pl.multiple_of(s * NP, NP)
-                for lb in range(2, 4):
-                    cols = slice(128 * lb, 128 * lb + 128)
-                    span = pl.ds(base, NP)
-                    state[lb, span, :] = state[lb, span, :] * keep_row[:, cols] + r_late[lb - 2, pl.ds(s, 1), :]
-                return carry
-
-            lax.fori_loop(0, NS, relax, 0)
             stores = [
                 pltpu.make_async_copy(
                     made.at[pl.ds(SPAN * k, SPAN)], parts_out.at[pl.ds(SPAN * k, SPAN)], store_sem.at[k]
@@ -407,9 +414,9 @@
                 for k in range(ROWS // SPAN)
             ]
             for k in range(ROWS // SPAN):
-                block = [rows_of(state, 4, SPAN * k, SPAN), rows_of(guest, 2, SPAN * k, SPAN)]
-                hi, lo = split(jnp.concatenate(block, axis=1))
-                made[SPAN * k : SPAN * k + SPAN, :] = mat(hi, final[...]) + mat(lo, final[...])
+                hi, lo = split(rows_of(guest, 2, SPAN * k, SPAN))
+                landing = final[CELLS:, :]
+                made[SPAN * k : SPAN * k + SPAN, :] += mat(hi, landing) + mat(lo, landing)
                 stores[k].start()
         await_row(s_recv, t, sr_sem)
         grid = grid + unpacked(s_recv[t].reshape(PLACES // 2, 128), to_box[...])

time: 86.6 us -> 84.6 us (0.977)
  Pallas kernels: 79.2 us -> 77.1 us
    pallas_call x1, Pallas kernels: 79.2 us -> 77.1 us  [per_device(): pl.pallas_call(step_kernel, out_shape=(jax.ShapeDtypeStruct((4 * NS, 128)...]
where the time goes in v5:
time: 84.6 us; the launch traced here: 84.4 us
  Pallas kernels  77.1 us (91%)
  local copies, waits for them, and re-layouts  5.99 us (7%)
  between operations  1.29 us (2%)
    pallas_call x1, Pallas kernels, per_device(): pl.pallas_call(step_kernel, out_shape=(jax.ShapeDtypeStruct((4 * NS, 128)...  77.1 us
    unnamed x2, local copies, waits for them, and re-layouts  5.99 us

profile of v5, /device:TPU:1, one launch (start us, length us, event | category | flops | bytes accessed | tf_op | source)
XLA Modules:
  0.0 84.4 jit_solution(7185090295853035412)
XLA Ops:
  1.3 77.1 %step.1 = (f32[216,128]{1,0:T(8,128)}, f32[1728,512]{1,0:T(8,128)}) custom-call(f32[216,128]{1,0:T(8,128)} %bitcast.13, f32[4,128]{1,0:T(4,128)} %bitcast.16, f32[1728,512]{1,0:T(8,128)} %bitcast.11, s32[4,128]{1,0:T(4,128)} %bitcast.17, s32[4,128]{1,0:T(4,128)} %bitcast.18, f32[1,512]{1,0:T(1,128)} %bitcast.19, s32[32,512]{1,0:T(8,128)} %partner.1, ...), custom_call_target="tpu_custom_call" | custom-call | tf_op jit(solution)/shard_map/step/pallas_call | solution.py:453
  78.4 1.5 %copy.19 = f32[54,2,2,128]{3,2,1,0:T(2,128)} copy(f32[54,2,2,128]{3,2,1,0:T(2,128)} %bitcast.14) | data formatting | bytes 221184
  79.9 4.4 %copy.20 = f32[54,32,512]{2,1,0:T(8,128)} copy(f32[54,32,512]{2,1,0:T(8,128)} %bitcast.12) | data formatting | bytes 7077888

commit v6 on v5

--- a/solution.py
+++ b/solution.py
@@ -17,9 +17,9 @@
 PLACES = 2 * OWNERS * HALF
 LIST = 256
 SPAN = 432
-STRIDE = 37
-EARLY = 90
-PACE = (30, 60)
+STRIDE = 43
+EARLY = 110
+PACE = (20, 70)
 CHAINS, WIDE = 2, 4
 LABEL = 54
 VMEM_LIMIT = 56 * 1024 * 1024
@@ -297,6 +297,10 @@
         copy.wait()
     for lb in range(2):
         mix(state, lb, partner[:, 128 * lb : 128 * lb + 128])
+    def with_source(grid, t):
+        await_row(s_recv, t, sr_sem)
+        return grid + unpacked(s_recv[t].reshape(PLACES // 2, 128), to_box[...])
+
     row = iota((64, CELLS), 0)
     for t in range(2):
         if t == 1:
@@ -398,6 +402,9 @@
                 hi, lo = split(rows_of(state, 4, SPAN * k, SPAN))
                 own = final[0:CELLS, :]
                 made[SPAN * k : SPAN * k + SPAN, :] = mat(hi, own) + mat(lo, own)
+            grid = with_source(grid, t)
+            for q in range(4):
+                grid_out[pl.ds(q, NS, stride=4), :] = grid[0:NS, 128 * q : 128 * q + 128]
             await_cells(moved, 1, move_recv.at[1])
             await_cells(r_moved, 1, move_recv.at[3])
             late_meta, _ = unpack_cells(1)
@@ -418,17 +425,13 @@
                 landing = final[CELLS:, :]
                 made[SPAN * k : SPAN * k + SPAN, :] += mat(hi, landing) + mat(lo, landing)
                 stores[k].start()
-        await_row(s_recv, t, sr_sem)
-        grid = grid + unpacked(s_recv[t].reshape(PLACES // 2, 128), to_box[...])
         if t == 0:
+            grid = with_source(grid, t)
             for q in range(4):
                 faces[1, q // 2, q % 2] = grid[0:56, 128 * q : 128 * q + 128]
             for copy in halos[1]:
                 copy.start()
             exchange_all(moving, moved, 1, 1, 1, PACE[0])
-        else:
-            for q in range(4):
-                grid_out[pl.ds(q, NS, stride=4), :] = grid[0:NS, 128 * q : 128 * q + 128]
     for copy in stores:
         copy.wait()
     for t in range(2):

time: 84.6 us -> 88.6 us (1.047)
  Pallas kernels: 77.1 us -> 81.2 us
    pallas_call x1, Pallas kernels: 77.1 us -> 81.2 us  [per_device(): pl.pallas_call(step_kernel, out_shape=(jax.ShapeDtypeStruct((4 * NS, 128)...]
where the time goes in v6:
time: 88.6 us; the launch traced here: 88.4 us
  Pallas kernels  81.2 us (92%)
  local copies, waits for them, and re-layouts  5.99 us (7%)
  between operations  1.29 us (1%)
    pallas_call x1, Pallas kernels, per_device(): pl.pallas_call(step_kernel, out_shape=(jax.ShapeDtypeStruct((4 * NS, 128)...  81.2 us
    unnamed x2, local copies, waits for them, and re-layouts  5.99 us

profile of v6, /device:TPU:1, one launch (start us, length us, event | category | flops | bytes accessed | tf_op | source)
XLA Modules:
  0.0 88.4 jit_solution(329463116073122665)
XLA Ops:
  1.3 81.2 %step.1 = (f32[216,128]{1,0:T(8,128)}, f32[1728,512]{1,0:T(8,128)}) custom-call(f32[216,128]{1,0:T(8,128)} %bitcast.13, f32[4,128]{1,0:T(4,128)} %bitcast.16, f32[1728,512]{1,0:T(8,128)} %bitcast.11, s32[4,128]{1,0:T(4,128)} %bitcast.17, s32[4,128]{1,0:T(4,128)} %bitcast.18, f32[1,512]{1,0:T(1,128)} %bitcast.19, s32[32,512]{1,0:T(8,128)} %partner.1, ...), custom_call_target="tpu_custom_call" | custom-call | tf_op jit(solution)/shard_map/step/pallas_call | solution.py:456
  82.4 1.5 %copy.19 = f32[54,2,2,128]{3,2,1,0:T(2,128)} copy(f32[54,2,2,128]{3,2,1,0:T(2,128)} %bitcast.14) | data formatting | bytes 221184
  84.0 4.4 %copy.20 = f32[54,32,512]{2,1,0:T(8,128)} copy(f32[54,32,512]{2,1,0:T(8,128)} %bitcast.12) | data formatting | bytes 7077888

commit v7 on v5

--- a/solution.py
+++ b/solution.py
@@ -17,9 +17,9 @@
 PLACES = 2 * OWNERS * HALF
 LIST = 256
 SPAN = 432
-STRIDE = 37
-EARLY = 90
-PACE = (30, 60)
+STRIDE = 43
+EARLY = 110
+PACE = (20, 70)
 CHAINS, WIDE = 2, 4
 LABEL = 54
 VMEM_LIMIT = 56 * 1024 * 1024

time: 84.6 us -> 84.8 us (level)
  no operation moved by 1% of the time
where the time goes in v7:
time: 84.8 us; the launch traced here: 84.6 us
  Pallas kernels  77.4 us (91%)
  local copies, waits for them, and re-layouts  5.99 us (7%)
  between operations  1.29 us (2%)
    pallas_call x1, Pallas kernels, per_device(): pl.pallas_call(step_kernel, out_shape=(jax.ShapeDtypeStruct((4 * NS, 128)...  77.4 us
    unnamed x2, local copies, waits for them, and re-layouts  5.99 us

profile of v7, /device:TPU:1, one launch (start us, length us, event | category | flops | bytes accessed | tf_op | source)
XLA Modules:
  0.0 84.6 jit_solution(15103333192123390620)
XLA Ops:
  1.3 77.4 %step.1 = (f32[216,128]{1,0:T(8,128)}, f32[1728,512]{1,0:T(8,128)}) custom-call(f32[216,128]{1,0:T(8,128)} %bitcast.13, f32[4,128]{1,0:T(4,128)} %bitcast.16, f32[1728,512]{1,0:T(8,128)} %bitcast.11, s32[4,128]{1,0:T(4,128)} %bitcast.17, s32[4,128]{1,0:T(4,128)} %bitcast.18, f32[1,512]{1,0:T(1,128)} %bitcast.19, s32[32,512]{1,0:T(8,128)} %partner.1, ...), custom_call_target="tpu_custom_call" | custom-call | tf_op jit(solution)/shard_map/step/pallas_call | solution.py:453
  78.7 1.5 %copy.19 = f32[54,2,2,128]{3,2,1,0:T(2,128)} copy(f32[54,2,2,128]{3,2,1,0:T(2,128)} %bitcast.14) | data formatting | bytes 221184
  80.2 4.4 %copy.20 = f32[54,32,512]{2,1,0:T(8,128)} copy(f32[54,32,512]{2,1,0:T(8,128)} %bitcast.12) | data formatting | bytes 7077888
